TPU v7x, 32 devices: a whole 2x2x4 slice. The times are simulated.
32 devices in a mesh: groups: 2 (over y), row: 4 (over z), chan: 2 (over x), sub: 2 (over core).
Axes of the slice: x: 2, y: 2, z: 4, core: 2. Of those that a mesh axis runs over, the one named last changes fastest.
Arguments:
- pair: bfloat16 [64, 32, 128], P(('groups', 'row'), ('chan', 'sub')), parts along dimension 0, may hold values from -8 to 8
- cotangent: bfloat16 [64, 32, 128], P(('groups', 'row'), ('chan', 'sub')), parts along dimension 0, may hold values from -6 to 6
- token_mask: int32 [64], P('groups'), parts along dimension 0, may hold values 0 or 1
- w_in: bfloat16 [2, 128, 640], replicated, may hold values from -0.5 to 0.5
- w_out: bfloat16 [2, 128, 128], replicated, may hold values from -0.5 to 0.5
Outputs:
- updated: bfloat16 [64, 32, 128], P(('groups', 'row'), ('chan', 'sub')), parts along dimension 0
- pair_grad: bfloat16 [64, 32, 128], P(('groups', 'row'), ('chan', 'sub')), parts along dimension 0
- grad_w_in: float32 [4, 128, 640], P('groups'), parts along dimension 0
- grad_w_out: float32 [4, 128, 128], P('groups'), parts along dimension 0
There are 2 independent parts, one for each index of `groups`. A program takes and returns all parts, laid end to end along the dimension named above; an argument that names none is the same for every part. Nothing has to cross between parts.
All inputs are finite; a program needn't handle non-finite values.
Results may differ from a plain program's by a relative error of at most 0.013.
Values may be sent and summed in bfloat16 or wider, within the bound.
No kernel may reach another device: no remote copies, remote signals or barrier semaphores. Data moves between devices by JAX's collectives and lax.ppermute only.
A program may use at most 64 MiB of HBM per device.

v0:
```python
import jax
import jax.numpy as jnp
from jax import lax
from jax.sharding import PartitionSpec as P

EPSILON = 1e-05


def layer_norm(values, norm_axis):
    centre = jnp.mean(values, axis=norm_axis, keepdims=True)
    shifted = values - centre
    spread = jnp.mean(shifted * shifted, axis=norm_axis, keepdims=True)
    inverse = lax.rsqrt(spread + EPSILON)
    return (shifted * inverse, inverse)


def norm_grad(upstream, normed, inverse, norm_axis):
    return inverse * (
        upstream
        - jnp.mean(upstream, axis=norm_axis, keepdims=True)
        - normed * jnp.mean(upstream * normed, axis=norm_axis, keepdims=True)
    )


def product_of(pattern, left_op, right_op):
    return jnp.einsum(pattern, left_op, right_op, preferred_element_type=jnp.float32)


def split_weights(w_in_u, hidden):
    channels = w_in_u.shape[0]
    return (w_in_u[:, : 4 * hidden].reshape(channels, 4, hidden), w_in_u[:, 4 * hidden :])


def front_block(state_block, rows_mask, cols_mask, w_in_u, hidden):
    normed, _ = layer_norm(state_block.astype(jnp.float32), -1)
    normed = normed.astype(jnp.bfloat16)
    w_pairs, w_gate = split_weights(w_in_u, hidden)
    projected = product_of("rjc,cke->kerj", normed, w_pairs)
    pair_mask = rows_mask[:, None] * cols_mask[None, :]
    left_side = jax.nn.sigmoid(projected[1]) * projected[0] * pair_mask
    right_side = jax.nn.sigmoid(projected[3]) * projected[2] * pair_mask
    return jnp.stack([left_side, right_side]).astype(jnp.bfloat16)


def back_block(state_block, tri_block, w_in_u, w_out_u, hidden):
    normed, _ = layer_norm(state_block.astype(jnp.float32), -1)
    normed = normed.astype(jnp.bfloat16)
    _, w_gate = split_weights(w_in_u, hidden)
    gate_value = jax.nn.sigmoid(product_of("rjc,cd->rjd", normed, w_gate))
    tnorm, _ = layer_norm(tri_block.astype(jnp.float32), 0)
    linear = product_of("erj,ec->rjc", tnorm.astype(jnp.bfloat16), w_out_u)
    return (state_block.astype(jnp.float32) + gate_value * linear).astype(jnp.bfloat16)


def grad_back_block(state_block, tri_block, upstream, w_in_u, w_out_u, hidden):
    normed, _ = layer_norm(state_block.astype(jnp.float32), -1)
    normed = normed.astype(jnp.bfloat16)
    _, w_gate = split_weights(w_in_u, hidden)
    gate_value = jax.nn.sigmoid(product_of("rjc,cd->rjd", normed, w_gate))
    tnorm, inverse = layer_norm(tri_block.astype(jnp.float32), 0)
    tnorm_low = tnorm.astype(jnp.bfloat16)
    grad_hidden = (upstream * gate_value).astype(jnp.bfloat16)
    wo_term = product_of("erj,rjc->ec", tnorm_low, grad_hidden)
    grad_tn = product_of("rjc,ec->erj", grad_hidden, w_out_u)
    grad_tri = norm_grad(grad_tn, tnorm, inverse, 0).astype(jnp.bfloat16)
    return (grad_tri, wo_term)


def grad_front_block(
    state_block, tri_block, grad_pairs, upstream, rows_mask, cols_mask, w_in_u, w_out_u, hidden
):
    normed_full, inverse = layer_norm(state_block.astype(jnp.float32), -1)
    normed = normed_full.astype(jnp.bfloat16)
    w_pairs, w_gate = split_weights(w_in_u, hidden)
    projected = product_of("rjc,cke->kerj", normed, w_pairs)
    gate_value = jax.nn.sigmoid(product_of("rjc,cd->rjd", normed, w_gate))
    tnorm, _ = layer_norm(tri_block.astype(jnp.float32), 0)
    linear = product_of("erj,ec->rjc", tnorm.astype(jnp.bfloat16), w_out_u)
    grad_gate = (upstream * linear * gate_value * (1.0 - gate_value)).astype(jnp.bfloat16)
    pair_mask = rows_mask[:, None] * cols_mask[None, :]
    sig_left = jax.nn.sigmoid(projected[1])
    sig_right = jax.nn.sigmoid(projected[3])
    grad_left = grad_pairs[0].astype(jnp.float32) * pair_mask
    grad_right = grad_pairs[1].astype(jnp.float32) * pair_mask
    grad_proj = jnp.stack(
        [
            grad_left * sig_left,
            grad_left * projected[0] * sig_left * (1.0 - sig_left),
            grad_right * sig_right,
            grad_right * projected[2] * sig_right * (1.0 - sig_right),
        ]
    ).astype(jnp.bfloat16)
    channels = state_block.shape[2]
    pair_term = product_of("rjc,kerj->cke", normed, grad_proj).reshape(channels, 4 * hidden)
    gate_term = product_of("rjc,rjd->cd", normed, grad_gate)
    wi_term = jnp.concatenate([pair_term, gate_term], axis=1)
    grad_normed = product_of("kerj,cke->rjc", grad_proj, w_pairs) + product_of(
        "rjd,cd->rjc", grad_gate, w_gate
    )
    grad_x = upstream + norm_grad(grad_normed, normed_full, inverse, -1)
    return (grad_x, wi_term)


def to_channels(stacked):
    return lax.all_to_all(stacked, ("chan", "sub"), split_axis=1, concat_axis=3, tiled=True)


def to_columns(stacked):
    return lax.all_to_all(stacked, ("chan", "sub"), split_axis=3, concat_axis=1, tiled=True)


def turn_rows(matrix):
    return lax.all_to_all(matrix, "row", split_axis=2, concat_axis=1, tiled=True)


def fold_rows(source, folder, initial):
    return folder(initial, lax.all_gather(source, "row", axis=1, tiled=True), jnp.int32(0))


def shards(pair, cotangent, token_mask, w_in, w_out):
    row_count, col_count, _ = pair.shape
    hidden = w_out.shape[1]
    token_total = token_mask.shape[0]
    row_id = lax.axis_index("row")
    col_id = lax.axis_index(("chan", "sub"))
    mask_full = token_mask.astype(jnp.float32)
    rows_mask = lax.dynamic_slice_in_dim(mask_full, row_id * row_count, row_count)
    cols_mask = lax.dynamic_slice_in_dim(mask_full, col_id * col_count, col_count)
    states = [pair]
    saved = []
    for layer_id in range(2):
        current = states[-1]
        pairs_local = front_block(current, rows_mask, cols_mask, w_in[layer_id], hidden)
        spread = to_channels(pairs_local)
        left_rows = spread[0]
        right_rows = spread[1]
        zero_tri = jnp.zeros(left_rows.shape, jnp.float32)
        keeper = None
        if layer_id == 0:

            def out_forward(totals, portion, offset):
                product_block = product_of("qrk,qjk->qrj", left_rows, portion)
                return product_block

            tri_rows = fold_rows(right_rows, out_forward, zero_tri)
        else:
            left_turned = turn_rows(left_rows)

            def in_forward(totals, portion, offset):
                return product_of("qki,qkj->qij", left_turned, portion)

            tri_rows = fold_rows(right_rows, in_forward, zero_tri)
        tri_cols = to_columns(tri_rows.astype(jnp.bfloat16)[None])[0]
        states.append(back_block(current, tri_cols, w_in[layer_id], w_out[layer_id], hidden))
        saved.append((left_rows, right_rows, tri_cols, keeper))
    upstream = cotangent.astype(jnp.float32)
    wi_grads = [None, None]
    wo_grads = [None, None]
    for layer_id in (1, 0):
        left_rows, right_rows, tri_cols, keeper = saved[layer_id]
        current = states[layer_id]
        grad_tri, wo_term = grad_back_block(
            current, tri_cols, upstream, w_in[layer_id], w_out[layer_id], hidden
        )
        grad_rows = to_channels(grad_tri[None])[0]
        zero_grad = jnp.zeros(left_rows.shape, jnp.float32)
        if layer_id == 1:

            def in_backward(carried, portion, offset):
                left_block = product_of("qkj,qij->qki", right_rows, portion)
                return (left_block, product_of("qki,qij->qkj", left_rows, portion))

            grad_left, grad_right = fold_rows(grad_rows, in_backward, (zero_grad, zero_grad))
        else:
            grad_turned = turn_rows(grad_rows)

            def right_step(totals, portion, offset):
                return product_of("qij,qik->qjk", grad_turned, portion)

            def left_step(totals, portion, offset):
                return product_of("qij,qjk->qik", grad_rows, portion)

            grad_left = fold_rows(right_rows, left_step, zero_grad)
            grad_right = fold_rows(left_rows, right_step, zero_grad)
        grad_pairs = to_columns(jnp.stack([grad_left, grad_right]).astype(jnp.bfloat16))
        upstream, wi_term = grad_front_block(
            current,
            tri_cols,
            grad_pairs,
            upstream,
            rows_mask,
            cols_mask,
            w_in[layer_id],
            w_out[layer_id],
            hidden,
        )
        wi_grads[layer_id] = wi_term
        wo_grads[layer_id] = wo_term
    wi_sum, wo_sum = lax.psum((jnp.stack(wi_grads), jnp.stack(wo_grads)), ("row", "chan", "sub"))
    return (states[2], upstream.astype(jnp.bfloat16), wi_sum / token_total, wo_sum / token_total)


def solution(mesh):
    placed = (
        P(("groups", "row"), ("chan", "sub"), None),
        P(("groups", "row"), ("chan", "sub"), None),
        P("groups"),
        P(),
        P(),
    )
    return jax.shard_map(
        shards,
        mesh=mesh,
        in_specs=placed,
        out_specs=(
            P(("groups", "row"), ("chan", "sub"), None),
            P(("groups", "row"), ("chan", "sub"), None),
            P("groups", None, None),
            P("groups", None, None),
        ),
        check_vma=False,
    )
```

profile of v0, /device:TPU:0, one launch (start us, length us, event | category | flops | bytes accessed | tf_op | source)
XLA Modules:
  0.0 252.0 jit_solution(1971059876714684459)
XLA Ops:
  7.2 1.0 slice_bitcast_fusion
  10.6 8.0 %all_to_all.144 = bf16[4,2,2048]{2,1,0:T(2,128)(2,1)S(1)} all-to-all(bf16[4,2,2048]{2,1,0:T(2,128)(2,1)S(1)} %reshape.259), channel_id=1, replica_groups=mesh['groups'=2,'row'=4,'chan'=2,'sub'=2] {'chan','sub'}, dimensions={0} | all-to-all | bytes 65536 | tf_op jit(solution)/shard_map/all_to_all | solution.py:105
  20.1 13.0 %all_gather.13 = bf16[32,32,32]{2,1,0:T(8,128)(2,1)S(1)} all-gather(bf16[32,8,32]{2,1,0:T(8,128)(2,1)S(1)} %copy.234), channel_id=1, replica_groups=mesh['groups'=2,'row'=4,'chan'=2,'sub'=2] {'row'}, dimensions={1}, use_global_device_ids=true | all-gather | bytes 81920 | tf_op jit(solution)/shard_map/all_gather | solution.py:117
  33.6 6.2 %all_to_all.145 = bf16[4,2,1024]{2,1,0:T(2,128)(2,1)S(1)} all-to-all(bf16[4,2,1024]{2,1,0:T(2,128)(2,1)S(1)} %reshape.261), channel_id=1, replica_groups=mesh['groups'=2,'row'=4,'chan'=2,'sub'=2] {'chan','sub'}, dimensions={0} | all-to-all | bytes 32768 | tf_op jit(solution)/shard_map/all_to_all | solution.py:109
  42.5 1.1 reshape.263
  43.7 3.3 %all-to-all-start.2 = ((bf16[4,2,2048]{2,1,0:T(2,128)(2,1)}), bf16[4,2,2048]{2,1,0:T(2,128)(2,1)S(1)}, u32[]{:S(2)}, u32[]{:S(2)}) async-start(bf16[4,2,2048]{2,1,0:T(2,128)(2,1)} %reshape.263), calls=%async_computation.2 | async-start | bytes 65536 | tf_op jit(solution)/shard_map/all_to_all | solution.py:105
  46.9 13.0 %all_gather.16 = bf16[32,32,32]{2,1,0:T(8,128)(2,1)S(1)} all-gather(bf16[32,8,32]{2,1,0:T(8,128)(2,1)S(1)} %copy.235), channel_id=1, replica_groups=mesh['groups'=2,'row'=4,'chan'=2,'sub'=2] {'row'}, dimensions={1}, use_global_device_ids=true | all-gather | bytes 81920 | tf_op jit(solution)/shard_map/all_gather | solution.py:117
  61.9 3.3 %all-to-all-start.3 = ((bf16[4,2,1024]{2,1,0:T(2,128)(2,1)}), bf16[4,2,1024]{2,1,0:T(2,128)(2,1)S(1)}, u32[]{:S(2)}, u32[]{:S(2)}) async-start(bf16[4,2,1024]{2,1,0:T(2,128)(2,1)} %reshape.265), calls=%async_computation.3 | async-start | bytes 32768 | tf_op jit(solution)/shard_map/all_to_all | solution.py:113
  65.3 13.9 %all_gather.14 = bf16[32,32,32]{2,1,0:T(8,128)(2,1)S(1)} all-gather(bf16[32,8,32]{2,1,0:T(8,128)(2,1)S(1)} %copy.247), channel_id=1, replica_groups=mesh['groups'=2,'row'=4,'chan'=2,'sub'=2] {'row'}, dimensions={1}, use_global_device_ids=true | all-gather | bytes 81920 | tf_op jit(solution)/shard_map/all_gather | solution.py:117
  80.6 3.3 %all-to-all-start.4 = ((bf16[4,2,1024]{2,1,0:T(2,128)(2,1)}), bf16[4,2,1024]{2,1,0:T(2,128)(2,1)S(1)}, u32[]{:S(2)}, u32[]{:S(2)}) async-start(bf16[4,2,1024]{2,1,0:T(2,128)(2,1)} %reshape.267), calls=%async_computation.4 | async-start | bytes 32768 | tf_op jit(solution)/shard_map/all_to_all | solution.py:109
  84.1 3.5 %all-to-all-done.4 = bf16[4,2,1024]{2,1,0:T(2,128)(2,1)S(1)} async-done(((bf16[4,2,1024]{2,1,0:T(2,128)(2,1)}), bf16[4,2,1024]{2,1,0:T(2,128)(2,1)S(1)}, u32[]{:S(2)}, u32[]{:S(2)}) %all-to-all-start.4) | async-done | bytes 16416 | tf_op jit(solution)/shard_map/all_to_all | solution.py:109
  91.5 3.3 %all-to-all-start.5 = ((bf16[4,2,1024]{2,1,0:T(2,128)(2,1)}), bf16[4,2,1024]{2,1,0:T(2,128)(2,1)S(1)}, u32[]{:S(2)}, u32[]{:S(2)}) async-start(bf16[4,2,1024]{2,1,0:T(2,128)(2,1)} %reshape.269), calls=%async_computation.5 | async-start | bytes 32768 | tf_op jit(solution)/shard_map/all_to_all | solution.py:105
  95.0 3.5 %all-to-all-done.5 = bf16[4,2,1024]{2,1,0:T(2,128)(2,1)S(1)} async-done(((bf16[4,2,1024]{2,1,0:T(2,128)(2,1)}), bf16[4,2,1024]{2,1,0:T(2,128)(2,1)S(1)}, u32[]{:S(2)}, u32[]{:S(2)}) %all-to-all-start.5) | async-done | bytes 16416 | tf_op jit(solution)/shard_map/all_to_all | solution.py:105
  99.3 13.3 %all_gather.15 = bf16[32,32,32]{2,1,0:T(8,128)(2,1)S(1)} all-gather(bf16[32,8,32]{2,1,0:T(8,128)(2,1)S(1)} %copy.256), channel_id=1, replica_groups=mesh['groups'=2,'row'=4,'chan'=2,'sub'=2] {'row'}, dimensions={1}, use_global_device_ids=true | all-gather | bytes 81920 | tf_op jit(solution)/shard_map/all_gather | solution.py:117
  114.0 3.3 %all-to-all-start.6 = ((bf16[4,2,2048]{2,1,0:T(2,128)(2,1)}), bf16[4,2,2048]{2,1,0:T(2,128)(2,1)S(1)}, u32[]{:S(2)}, u32[]{:S(2)}) async-start(bf16[4,2,2048]{2,1,0:T(2,128)(2,1)} %reshape.271), calls=%async_computation.6 | async-start | bytes 65536 | tf_op jit(solution)/shard_map/all_to_all | solution.py:109
  117.6 3.6 %all-to-all-done.6 = bf16[4,2,2048]{2,1,0:T(2,128)(2,1)S(1)} async-done(((bf16[4,2,2048]{2,1,0:T(2,128)(2,1)}), bf16[4,2,2048]{2,1,0:T(2,128)(2,1)S(1)}, u32[]{:S(2)}, u32[]{:S(2)}) %all-to-all-start.6) | async-done | bytes 32800 | tf_op jit(solution)/shard_map/all_to_all | solution.py:109
  124.3 3.3 %all-to-all-start.7 = ((bf16[4,2,1024]{2,1,0:T(2,128)(2,1)}), bf16[4,2,1024]{2,1,0:T(2,128)(2,1)S(1)}, u32[]{:S(2)}, u32[]{:S(2)}) async-start(bf16[4,2,1024]{2,1,0:T(2,128)(2,1)} %reshape.273), calls=%async_computation.7 | async-start | bytes 32768 | tf_op jit(solution)/shard_map/all_to_all | solution.py:105
  128.1 3.4 %all-to-all-done.7 = bf16[4,2,1024]{2,1,0:T(2,128)(2,1)S(1)} async-done(((bf16[4,2,1024]{2,1,0:T(2,128)(2,1)}), bf16[4,2,1024]{2,1,0:T(2,128)(2,1)S(1)}, u32[]{:S(2)}, u32[]{:S(2)}) %all-to-all-start.7) | async-done | bytes 16416 | tf_op jit(solution)/shard_map/all_to_all | solution.py:105
  132.8 3.3 %all-to-all-start.8 = ((bf16[4,2,1024]{2,1,0:T(2,128)(2,1)}), bf16[4,2,1024]{2,1,0:T(2,128)(2,1)S(1)}, u32[]{:S(2)}, u32[]{:S(2)}) async-start(bf16[4,2,1024]{2,1,0:T(2,128)(2,1)} %reshape.275), calls=%async_computation.8 | async-start | bytes 32768 | tf_op jit(solution)/shard_map/all_to_all | solution.py:113
  136.4 5.3 %all-to-all-done.8 = bf16[4,2,1024]{2,1,0:T(2,128)(2,1)S(1)} async-done(((bf16[4,2,1024]{2,1,0:T(2,128)(2,1)}), bf16[4,2,1024]{2,1,0:T(2,128)(2,1)S(1)}, u32[]{:S(2)}, u32[]{:S(2)}) %all-to-all-start.8) | async-done | bytes 16416 | tf_op jit(solution)/shard_map/all_to_all | solution.py:113
  143.1 3.3 %all-to-all-start.9 = ((bf16[4,2,2048]{2,1,0:T(2,128)(2,1)}), bf16[4,2,2048]{2,1,0:T(2,128)(2,1)S(1)}, u32[]{:S(2)}, u32[]{:S(2)}) async-start(bf16[4,2,2048]{2,1,0:T(2,128)(2,1)} %reshape.277), calls=%async_computation.9 | async-start | bytes 65536 | tf_op jit(solution)/shard_map/all_to_all | solution.py:109
  147.1 3.2 %all-to-all-done.9 = bf16[4,2,2048]{2,1,0:T(2,128)(2,1)S(1)} async-done(((bf16[4,2,2048]{2,1,0:T(2,128)(2,1)}), bf16[4,2,2048]{2,1,0:T(2,128)(2,1)S(1)}, u32[]{:S(2)}, u32[]{:S(2)}) %all-to-all-start.9) | async-done | bytes 32800 | tf_op jit(solution)/shard_map/all_to_all | solution.py:109
  153.4 89.0 %all-reduce.3.cloned.1.call-done = (f32[2,128,640]{2,1,0:T(8,128)}, f32[2,128,128]{2,1,0:T(8,128)}) async-done(((f32[2,128,640]{2,1,0:T(8,128)}, f32[2,128,128]{2,1,0:T(8,128)}), (f32[2,128,640]{2,1,0:T(8,128)}, f32[2,128,128]{2,1,0:T(8,128)})) %all-reduce.3.cloned.1.call-update) | async-done | bytes 786448 | tf_op jit(solution)/shard_map/psum | solution.py:199
  242.5 2.0 broadcast_multiply_fusion
  (159 shorter events, 28.1 us)
Async XLA Ops:
  7.2 1.0 copy-start
  8.5 0.7 copy-start.4
  40.3 0.8 copy-start.1
  43.7 16.3 %all-to-all-start.2 = ((bf16[4,2,2048]{2,1,0:T(2,128)(2,1)}), bf16[4,2,2048]{2,1,0:T(2,128)(2,1)S(1)}, u32[]{:S(2)}, u32[]{:S(2)}) async-start(bf16[4,2,2048]{2,1,0:T(2,128)(2,1)} %reshape.263), calls=%async_computation.2 | async-start | bytes 65536 | tf_op jit(solution)/shard_map/all_to_all | solution.py:105
  61.9 17.3 %all-to-all-start.3 = ((bf16[4,2,1024]{2,1,0:T(2,128)(2,1)}), bf16[4,2,1024]{2,1,0:T(2,128)(2,1)S(1)}, u32[]{:S(2)}, u32[]{:S(2)}) async-start(bf16[4,2,1024]{2,1,0:T(2,128)(2,1)} %reshape.265), calls=%async_computation.3 | async-start | bytes 32768 | tf_op jit(solution)/shard_map/all_to_all | solution.py:113
  80.6 7.1 %all-to-all-start.4 = ((bf16[4,2,1024]{2,1,0:T(2,128)(2,1)}), bf16[4,2,1024]{2,1,0:T(2,128)(2,1)S(1)}, u32[]{:S(2)}, u32[]{:S(2)}) async-start(bf16[4,2,1024]{2,1,0:T(2,128)(2,1)} %reshape.267), calls=%async_computation.4 | async-start | bytes 32768 | tf_op jit(solution)/shard_map/all_to_all | solution.py:109
  88.5 0.7 copy-start.2
  91.5 7.1 %all-to-all-start.5 = ((bf16[4,2,1024]{2,1,0:T(2,128)(2,1)}), bf16[4,2,1024]{2,1,0:T(2,128)(2,1)S(1)}, u32[]{:S(2)}, u32[]{:S(2)}) async-start(bf16[4,2,1024]{2,1,0:T(2,128)(2,1)} %reshape.269), calls=%async_computation.5 | async-start | bytes 32768 | tf_op jit(solution)/shard_map/all_to_all | solution.py:105
  114.0 7.2 %all-to-all-start.6 = ((bf16[4,2,2048]{2,1,0:T(2,128)(2,1)}), bf16[4,2,2048]{2,1,0:T(2,128)(2,1)S(1)}, u32[]{:S(2)}, u32[]{:S(2)}) async-start(bf16[4,2,2048]{2,1,0:T(2,128)(2,1)} %reshape.271), calls=%async_computation.6 | async-start | bytes 65536 | tf_op jit(solution)/shard_map/all_to_all | solution.py:109
  124.3 7.1 %all-to-all-start.7 = ((bf16[4,2,1024]{2,1,0:T(2,128)(2,1)}), bf16[4,2,1024]{2,1,0:T(2,128)(2,1)S(1)}, u32[]{:S(2)}, u32[]{:S(2)}) async-start(bf16[4,2,1024]{2,1,0:T(2,128)(2,1)} %reshape.273), calls=%async_computation.7 | async-start | bytes 32768 | tf_op jit(solution)/shard_map/all_to_all | solution.py:105
  132.8 8.8 %all-to-all-start.8 = ((bf16[4,2,1024]{2,1,0:T(2,128)(2,1)}), bf16[4,2,1024]{2,1,0:T(2,128)(2,1)S(1)}, u32[]{:S(2)}, u32[]{:S(2)}) async-start(bf16[4,2,1024]{2,1,0:T(2,128)(2,1)} %reshape.275), calls=%async_computation.8 | async-start | bytes 32768 | tf_op jit(solution)/shard_map/all_to_all | solution.py:113
  143.1 7.2 %all-to-all-start.9 = ((bf16[4,2,2048]{2,1,0:T(2,128)(2,1)}), bf16[4,2,2048]{2,1,0:T(2,128)(2,1)S(1)}, u32[]{:S(2)}, u32[]{:S(2)}) async-start(bf16[4,2,2048]{2,1,0:T(2,128)(2,1)} %reshape.277), calls=%async_computation.9 | async-start | bytes 65536 | tf_op jit(solution)/shard_map/all_to_all | solution.py:109
  146.4 96.1 %all-reduce.3.cloned.1.call-start = ((), (), s32[]{:S(2)}) async-start(), calls=%async_computation.10 | async-start | bytes 1572864 | tf_op jit(solution)/shard_map/psum | solution.py:199
  242.5 2.0 copy-start.3
Sparse Core Ops, SparseCore 0:
  152.8 89.6 all-reduce.2
where the time goes:
time: 253 us; the launch traced here: 252 us
  waiting for transfers between devices  112 us (44%)
  blocking collectives  67.3 us (27%)
  starting transfers between devices  26.1 us (10%)
  local copies, waits for them, and re-layouts  19.2 us (8%)
  between operations  14.8 us (6%)
  other arithmetic  7.05 us (3%)
  matrix products  5.95 us (2%)
    psum x1, waiting for transfers between devices, shards(): lax.psum((jnp.stack(wi_grads), jnp.stack(wo_grads)), ('row', 'chan', 'sub'))  89 us
    all_gather x4, blocking collectives, fold_rows(): lax.all_gather(source, 'row', axis=1, tiled=True)  53.2 us
    unnamed x31, local copies, waits for them, and re-layouts  11.8 us
    all_to_all x3, waiting for transfers between devices, to_columns(): lax.all_to_all(stacked, ('chan', 'sub'), split_axis=3, concat_axis=1, til...  10.3 us
    all_to_all x3, starting transfers between devices, to_columns(): lax.all_to_all(stacked, ('chan', 'sub'), split_axis=3, concat_axis=1, til...  9.78 us
    all_to_all x3, starting transfers between devices, to_channels(): lax.all_to_all(stacked, ('chan', 'sub'), split_axis=1, concat_axis=3, til...  9.77 us
    all_to_all x1, blocking collectives, to_channels(): lax.all_to_all(stacked, ('chan', 'sub'), split_axis=1, concat_axis=3, til...  7.95 us
    all_to_all x3, waiting for transfers between devices, to_channels(): lax.all_to_all(stacked, ('chan', 'sub'), split_axis=1, concat_axis=3, til...  6.91 us
  transfers between devices with their start and end apart: 9, of which 7 were waited for; matrix products, arithmetic and copies ran while one was open for 1% of the time, Pallas kernels for 0%

commit v1 on v0

--- a/solution.py
+++ b/solution.py
@@ -1,9 +1,284 @@
+import functools
+
 import jax
 import jax.numpy as jnp
 from jax import lax
+from jax.experimental import pallas as pl
+from jax.experimental.pallas import tpu as pltpu
 from jax.sharding import PartitionSpec as P
 
 EPSILON = 1e-05
+F32 = jnp.float32
+BF16 = jnp.bfloat16
+TILE = 8
+PLANES = 40
+VMEM_BYTES = 56 * 2**20
+VMEM_PLAN = 40 * 2**20
+
+
+def dot(left, right):
+    return lax.dot_general(left, right, (((1,), (0,)), ((), ())), preferred_element_type=F32)
+
+
+def dot_rows(left, right):
+    return lax.dot_general(left, right, (((0,), (0,)), ((), ())), preferred_element_type=F32)
+
+
+def dot_last(left, right):
+    return lax.dot_general(left, right, (((1,), (1,)), ((), ())), preferred_element_type=F32)
+
+
+def lane_mean(values):
+    return jnp.mean(values, axis=-1, keepdims=True)
+
+
+def norm_of(values):
+    shifted = values - lane_mean(values)
+    inverse = lax.rsqrt(lane_mean(shifted * shifted) + EPSILON)
+    return shifted * inverse, inverse
+
+
+def norm_back(upstream, normed, inverse):
+    return inverse * (upstream - lane_mean(upstream) - normed * lane_mean(upstream * normed))
+
+
+def sigmoid(values):
+    return 0.5 * jnp.tanh(0.5 * values) + 0.5
+
+
+def rounded(values):
+    return values.astype(BF16).astype(F32)
+
+
+def triangle(tokens, left, left_row, right, right_turned, store, group):
+    tiles = tokens // TILE
+
+    def right_tile(r, q):
+        if right_turned:
+            return right[pl.ds(q * TILE * tokens + r, TILE, stride=tokens), :]
+        return right[pl.ds(r * tokens + q * TILE, TILE), :]
+
+    def body(step, carry):
+        first = step * group
+        totals = [[None] * tiles for _ in range(group)]
+        for r in range(tokens):
+            column = [right_tile(r, q) for q in range(tiles)]
+            for g in range(group):
+                scale = jnp.broadcast_to(left[pl.ds(left_row(first + g, r), 1), :], column[0].shape)
+                for q in range(tiles):
+                    term = scale * column[q]
+                    totals[g][q] = term if r == 0 else totals[g][q] + term
+        for g in range(group):
+            store(first + g, totals[g])
+        return carry
+
+    lax.fori_loop(0, tokens // group, body, 0)
+
+
+def whole_kernel(
+    tokens, sizes, chunk, group, parts_ref, mask_ref, w_in_ref, w_out_ref,
+    updated_ref, pair_grad_ref, gwi_ref, gwo_ref,
+    states, cot, flat, side, normed, inv, normed16, one_a, two_a, one_b, two_b, gate, tnorm, tinv, tnorm16, linear,
+    tri, ga, gb, w_turned, wo_turned, gproj,
+):
+    n_row, n_chan, n_sub = sizes
+    row_id, chan_id, sub_id = lax.axis_index("row"), lax.axis_index("chan"), lax.axis_index("sub")
+    rows, cols = tokens // n_row, tokens // (n_chan * n_sub)
+    pairs = tokens * tokens
+    hidden = w_out_ref.shape[1]
+    channels = w_in_ref.shape[1]
+    steps = pairs // chunk
+    x_ref, gy_ref = states.at[0], cot
+
+    for s_row in range(n_row):
+        for s_chan in range(n_chan):
+            for s_sub in range(n_sub):
+                r0 = lax.rem(row_id + n_row - s_row, n_row) * rows
+                c0 = (lax.rem(chan_id + n_chan - s_chan, n_chan) * n_sub + lax.rem(sub_id + n_sub - s_sub, n_sub)) * cols
+                c0 = pl.multiple_of(c0, TILE)
+                for which, target in ((0, x_ref), (1, gy_ref)):
+                    block = parts_ref[s_row, s_chan, s_sub, which].astype(F32).reshape(rows, cols, channels)
+                    for r in range(rows):
+                        at = pl.multiple_of((r0 + r) * tokens + c0, TILE)
+                        target[pl.ds(at, cols), :] = block[r]
+
+    for u in range(2):
+        w_turned[u] = w_in_ref[u].T
+        wo_turned[u] = w_out_ref[u].T
+
+    def mask_of(step):
+        lines = chunk // tokens
+        outer = mask_ref[pl.ds(pl.multiple_of(step * lines, lines), lines), :]
+        full = mask_ref[...]
+        return (outer[:, None, :] * full[None, :, :]).reshape(chunk, channels)
+
+    def at_chunk(step):
+        return pl.ds(pl.multiple_of(step * chunk, chunk), chunk)
+
+    def front(u, x, step):
+        here = at_chunk(step)
+        n, s = norm_of(x)
+        normed[u, here, :] = n
+        inv[u, here, :] = jnp.broadcast_to(s, n.shape)
+        n16 = n.astype(BF16)
+        normed16[u, here, :] = n16
+        projected = dot(n16, w_in_ref[u])
+        pa, qa, pb, qb, qz = [projected[:, hidden * k : hidden * (k + 1)] for k in range(5)]
+        mask = mask_of(step)
+        for p, q, one, two, keep in ((pa, qa, one_a, two_a, flat), (pb, qb, one_b, two_b, side)):
+            sig = sigmoid(q)
+            first = sig * mask
+            value = first * p
+            one[u, here, :] = first
+            two[u, here, :] = value * (1.0 - sig)
+            keep[u, here, :] = rounded(value)
+        gate[u, here, :] = sigmoid(qz)
+
+    def back(u, step):
+        here = at_chunk(step)
+        tn, r = norm_of(rounded(tri[here, :]))
+        tnorm[u, here, :] = tn
+        tinv[u, here, :] = jnp.broadcast_to(r, tn.shape)
+        tn16 = tn.astype(BF16)
+        tnorm16[u, here, :] = tn16
+        lin = dot(tn16, w_out_ref[u])
+        linear[u, here, :] = lin
+        return rounded(states[u, here, :] + gate[u, here, :] * lin)
+
+    def grad_back(u, gy, step):
+        here = at_chunk(step)
+        gh = (gy * gate[u, here, :]).astype(BF16)
+        term = dot_rows(tnorm16[u, here, :], gh)
+        gwo_ref[u] = gwo_ref[u] + term
+        gtn = dot(gh, wo_turned[u])
+        tri[here, :] = rounded(norm_back(gtn, tnorm[u, here, :], tinv[u, here, :]))
+
+    def grad_front(u, gy, step, wants_all):
+        here = at_chunk(step)
+        z = gate[u, here, :]
+        ga16 = rounded(ga[here, :])
+        gb16 = rounded(gb[here, :])
+        pieces = [
+            ga16 * one_a[u, here, :],
+            ga16 * two_a[u, here, :],
+            gb16 * one_b[u, here, :],
+            gb16 * two_b[u, here, :],
+            gy * linear[u, here, :] * z * (1.0 - z),
+        ]
+        g = jnp.concatenate([p.astype(BF16) for p in pieces], axis=1)
+        gwi_ref[u] = gwi_ref[u] + dot_rows(normed16[u, here, :], g)
+        if not wants_all:
+            return None
+        h = dot(g, w_turned[u])
+        return gy + norm_back(h, normed[u, here, :], inv[u, here, :])
+
+    def loop(body):
+        def step_of(step, carry):
+            body(step)
+            return carry
+
+        lax.fori_loop(0, steps, step_of, 0)
+
+    def store_to(target):
+        def store(p, values):
+            for q, value in enumerate(values):
+                target[pl.ds(pl.multiple_of(p * tokens + q * TILE, TILE), TILE), :] = value
+
+        return store
+
+    natural = lambda p, r: p * tokens + r
+    turned = lambda p, r: r * tokens + p
+
+    gwi_ref[...] = jnp.zeros(gwi_ref.shape, F32)
+    gwo_ref[...] = jnp.zeros(gwo_ref.shape, F32)
+
+    loop(lambda step: front(0, states[0, at_chunk(step), :], step))
+    triangle(tokens, flat.at[0], natural, side.at[0], True, store_to(tri), group)
+
+    def middle(step):
+        x1 = back(0, step)
+        states[1, at_chunk(step), :] = x1
+        front(1, x1, step)
+
+    loop(middle)
+    triangle(tokens, flat.at[1], turned, side.at[1], False, store_to(tri), group)
+
+    def turn(step):
+        states[0, at_chunk(step), :] = back(1, step)
+        grad_back(1, gy_ref[at_chunk(step), :], step)
+
+    loop(turn)
+
+    triangle(tokens, side.at[1], natural, tri, True, store_to(ga), group)
+    triangle(tokens, flat.at[1], natural, tri, False, store_to(gb), group)
+
+    def down(step):
+        gx = grad_front(1, gy_ref[at_chunk(step), :], step, True)
+        gy_ref[at_chunk(step), :] = gx
+        grad_back(0, gx, step)
+
+    loop(down)
+    triangle(tokens, tri, natural, side.at[0], False, store_to(ga), group)
+    triangle(tokens, tri, turned, flat.at[0], False, store_to(gb), group)
+
+    def last(step):
+        gx = grad_front(0, gy_ref[at_chunk(step), :], step, True)
+        gy_ref[at_chunk(step), :] = gx
+
+    loop(last)
+    gwi_ref[...] = gwi_ref[...] * (1.0 / tokens)
+    gwo_ref[...] = gwo_ref[...] * (1.0 / tokens)
+
+    r0 = row_id * rows
+    c0 = pl.multiple_of((chan_id * n_sub + sub_id) * cols, TILE)
+    for source, target in ((states.at[0], updated_ref), (gy_ref, pair_grad_ref)):
+        for r in range(rows):
+            at = pl.multiple_of((r0 + r) * tokens + c0, TILE)
+            target[r] = source[pl.ds(at, cols), :].astype(BF16)
+
+
+def gather_part(pair, cotangent, sizes):
+    channels = pair.shape[-1]
+    block = jnp.stack([pair.reshape(-1, channels), cotangent.reshape(-1, channels)])
+    for axis, size in zip(("sub", "chan", "row"), sizes[::-1]):
+        moved = [block]
+        for shift in range(1, size):
+            moved.append(lax.ppermute(block, axis, [(i, (i + shift) % size) for i in range(size)]))
+        block = jnp.stack(moved)
+    return block
+
+
+def whole_part(sizes, pair, cotangent, token_mask, w_in, w_out):
+    tokens = token_mask.shape[0]
+    channels = pair.shape[-1]
+    hidden = w_out.shape[1]
+    pairs = tokens * tokens
+    parts = gather_part(pair, cotangent, sizes)
+    mask = jnp.broadcast_to(token_mask.astype(F32)[:, None], (tokens, channels))
+    chunk = 8 * tokens
+    plane = pltpu.VMEM((pairs, channels), F32)
+    two = pltpu.VMEM((2, pairs, channels), F32)
+    two16 = pltpu.VMEM((2, pairs, channels), BF16)
+    vmem = pl.BlockSpec(memory_space=pltpu.VMEM)
+    return pl.pallas_call(
+        functools.partial(whole_kernel, tokens, sizes, chunk, 8),
+        out_shape=(
+            jax.ShapeDtypeStruct(pair.shape, BF16),
+            jax.ShapeDtypeStruct(pair.shape, BF16),
+            jax.ShapeDtypeStruct(w_in.shape, F32),
+            jax.ShapeDtypeStruct(w_out.shape, F32),
+        ),
+        in_specs=[vmem] * 4,
+        out_specs=(vmem,) * 4,
+        scratch_shapes=[
+            two, plane, two, two, two, two, two16, two, two, two, two, two, two, two, two16, two,
+            plane, plane, plane,
+            pltpu.VMEM((2, w_in.shape[2], channels), BF16),
+            pltpu.VMEM((2, channels, hidden), BF16),
+            pltpu.VMEM((chunk, w_in.shape[2]), BF16),
+        ],
+        compiler_params=pltpu.CompilerParams(vmem_limit_bytes=VMEM_BYTES),
+    )(parts, mask, w_in, w_out)
 
 
 def layer_norm(values, norm_axis):
@@ -117,7 +392,7 @@
     return folder(initial, lax.all_gather(source, "row", axis=1, tiled=True), jnp.int32(0))
 
 
-def shards(pair, cotangent, token_mask, w_in, w_out):
+def spread_part(pair, cotangent, token_mask, w_in, w_out):
     row_count, col_count, _ = pair.shape
     hidden = w_out.shape[1]
     token_total = token_mask.shape[0]
@@ -201,6 +476,15 @@
 
 
 def solution(mesh):
+    sizes = tuple(mesh.shape[axis] for axis in ("row", "chan", "sub"))
+
+    def shards(pair, cotangent, token_mask, w_in, w_out):
+        tokens = token_mask.shape[0]
+        tiled = tokens % (TILE * sizes[1] * sizes[2]) == 0
+        if tiled and PLANES * tokens * tokens * pair.shape[-1] * 4 <= VMEM_PLAN:
+            return whole_part(sizes, pair, cotangent, token_mask, w_in, w_out)
+        return spread_part(pair, cotangent, token_mask, w_in, w_out)
+
     placed = (
         P(("groups", "row"), ("chan", "sub"), None),
         P(("groups", "row"), ("chan", "sub"), None),

time: 253 us -> 45.7 us (0.18)
  waiting for transfers between devices: 112 us -> 9.48 us
  blocking collectives: 67.3 us -> 0 us
  Pallas kernels: 0 us -> 22.8 us
  local copies, waits for them, and re-layouts: 19.2 us -> 0.67 us
  starting transfers between devices: 26.1 us -> 10.2 us
  between operations: 14.8 us -> 0.65 us
  matrix products: 5.95 us -> 0 us
  other arithmetic: 7.05 us -> 1.64 us
    psum x1 -> x0, waiting for transfers between devices: 89 us -> none  [shards(): lax.psum((jnp.stack(wi_grads), jnp.stack(wo_grads)), ('row', 'chan', 'sub'))]
    all_gather x4 -> x0, blocking collectives: 53.2 us -> none  [fold_rows(): lax.all_gather(source, 'row', axis=1, tiled=True)]
    all_to_all x8 -> x0, starting transfers between devices: 26.1 us -> none  [the longest x3 9.78 us: to_columns(): lax.all_to_all(stacked, ('chan', 'sub'), split_axis=3, concat_axis=1, til...]
    pallas_call x0 -> x1, Pallas kernels: none -> 22.8 us  [whole_part(): pl.pallas_call(functools.partial(whole_kernel, tokens, sizes, chunk, 8),...]
    all_to_all x8 -> x0, waiting for transfers between devices: 22.5 us -> none  [the longest x3 10.3 us: to_columns(): lax.all_to_all(stacked, ('chan', 'sub'), split_axis=3, concat_axis=1, til...]
    all_to_all x2 -> x0, blocking collectives: 14.2 us -> none  [the longest x1 7.95 us: to_channels(): lax.all_to_all(stacked, ('chan', 'sub'), split_axis=1, concat_axis=3, til...]
    unnamed x31 -> x2, local copies, waits for them, and re-layouts: 11.8 us -> 0.01 us
    ppermute x0 -> x5, starting transfers between devices: none -> 10.2 us  [gather_part(): lax.ppermute(block, axis, [(i, (i + shift) % size) for i in range(size)])]
  transfers between devices with their start and end apart: 9 -> 5, of which waited for: 7 -> 4; matrix products, arithmetic and copies ran while one was open for 1% -> 0% of each run, Pallas kernels for 0% -> 0%
where the time goes in v1:
time: 45.7 us; the launch traced here: 45.4 us
  Pallas kernels  22.8 us (50%)
  starting transfers between devices  10.2 us (22%)
  waiting for transfers between devices  9.48 us (21%)
  other arithmetic  1.64 us (4%)
  local copies, waits for them, and re-layouts  0.67 us (1%)
  between operations  0.65 us (1%)
    pallas_call x1, Pallas kernels, whole_part(): pl.pallas_call(functools.partial(whole_kernel, tokens, sizes, chunk, 8),...  22.8 us
    ppermute x5, starting transfers between devices, gather_part(): lax.ppermute(block, axis, [(i, (i + shift) % size) for i in range(size)])  10.2 us
    ppermute x5, waiting for transfers between devices, gather_part(): lax.ppermute(block, axis, [(i, (i + shift) % size) for i in range(size)])  9.48 us
    another operation x4, other arithmetic, gather_part(): block = jnp.stack(moved)  1.64 us
  transfers between devices with their start and end apart: 5, of which 4 were waited for; matrix products, arithmetic and copies ran while one was open for 0% of the time, Pallas kernels for 0%

profile of v1, /device:TPU:0, one launch (start us, length us, event | category | flops | bytes accessed | tf_op | source)
XLA Modules:
  0.0 45.4 jit_solution(11233497762419098198)
XLA Ops:
  0.6 0.7 %fusion = (bf16[1,2,64,128]{3,2,1,0:T(8,128)(2,1)S(1)}, bf16[2,64,128]{2,1,0:T(8,128)(2,1)S(1)}) fusion(bf16[1,64,128]{2,1,0:T(8,128)(2,1)} %bitcast.18, bf16[1,64,128]{2,1,0:T(8,128)(2,1)} %bitcast.19), kind=kLoop, calls=%fused_computation.4 | loop fusion | flops 16384 | bytes 98304 | tf_op jit(solution)/shard_map/stack | solution.py:247
  1.4 0.5 collective-permute-start
  1.8 0.9 %collective-permute-done = bf16[2,64,128]{2,1,0:T(8,128)(2,1)S(1)} collective-permute-done((bf16[2,64,128]{2,1,0:T(8,128)(2,1)S(1)}, bf16[2,64,128]{2,1,0:T(8,128)(2,1)S(1)}, u32[]{:S(2)}, u32[]{:S(2)}) %collective-permute-start) | collective-permute-done | bytes 32800 | tf_op jit(solution)/shard_map/ppermute | solution.py:246
  2.7 2.9 %collective-permute-start.1 = (bf16[2,2,64,128]{3,2,1,0:T(8,128)(2,1)S(1)}, bf16[2,2,64,128]{3,2,1,0:T(8,128)(2,1)S(1)}, u32[]{:S(2)}, u32[]{:S(2)}) collective-permute-start(bf16[2,2,64,128]{3,2,1,0:T(8,128)(2,1)S(1)} %get-tuple-element.7), channel_id=1, source_target_pairs={{0,2},{2,0},{1,3},{3,1},{4,6},{6,4},{5,7},{7,5},{8,10},{10,8},{9,1... | collective-permute-start | bytes 196616 | tf_op jit(solution)/shard_map/ppermute | solution.py:246
  5.6 2.4 %collective-permute-done.1 = bf16[2,2,64,128]{3,2,1,0:T(8,128)(2,1)S(1)} collective-permute-done((bf16[2,2,64,128]{3,2,1,0:T(8,128)(2,1)S(1)}, bf16[2,2,64,128]{3,2,1,0:T(8,128)(2,1)S(1)}, u32[]{:S(2)}, u32[]{:S(2)}) %collective-permute-start.1) | collective-permute-done | bytes 65568 | tf_op jit(solution)/shard_map/ppermute | solution.py:246
  8.0 0.0 copy-start
  8.1 3.0 %collective-permute-start.3 = (bf16[2,2,2,64,128]{4,3,2,1,0:T(8,128)(2,1)S(1)}, bf16[2,2,2,64,128]{4,3,2,1,0:T(8,128)(2,1)S(1)}, u32[]{:S(2)}, u32[]{:S(2)}) collective-permute-start(bf16[2,2,2,64,128]{4,3,2,1,0:T(8,128)(2,1)S(1)} %get-tuple-element.5), channel_id=1, source_target_pairs={{0,8},{4,12},{8,0},{12,4},{1,9},{5,13},{9,1},{13,5},{2,10},{6,14},... | collective-permute-start | bytes 393224 | tf_op jit(solution)/shard_map/ppermute | solution.py:246
  11.1 1.6 %collective-permute-start.2 = (bf16[2,2,2,64,128]{4,3,2,1,0:T(8,128)(2,1)S(1)}, bf16[2,2,2,64,128]{4,3,2,1,0:T(8,128)(2,1)S(1)}, u32[]{:S(2)}, u32[]{:S(2)}) collective-permute-start(bf16[2,2,2,64,128]{4,3,2,1,0:T(8,128)(2,1)S(1)} %get-tuple-element.5), channel_id=1, source_target_pairs={{0,4},{4,8},{8,12},{12,0},{1,5},{5,9},{9,13},{13,1},{2,6},{6,10},{... | collective-permute-start | bytes 393224 | tf_op jit(solution)/shard_map/ppermute | solution.py:246
  12.6 2.2 %collective-permute-start.4 = (bf16[2,2,2,64,128]{4,3,2,1,0:T(8,128)(2,1)S(1)}, bf16[2,2,2,64,128]{4,3,2,1,0:T(8,128)(2,1)S(1)}, u32[]{:S(2)}, u32[]{:S(2)}) collective-permute-start(bf16[2,2,2,64,128]{4,3,2,1,0:T(8,128)(2,1)S(1)} %get-tuple-element.5), channel_id=1, source_target_pairs={{0,12},{4,0},{8,4},{12,8},{1,13},{5,1},{9,5},{13,9},{2,14},{6,2},{... | collective-permute-start | bytes 393224 | tf_op jit(solution)/shard_map/ppermute | solution.py:246
  14.9 0.0 copy-done
  14.9 5.7 %collective-permute-done.3 = bf16[2,2,2,64,128]{4,3,2,1,0:T(8,128)(2,1)S(1)} collective-permute-done((bf16[2,2,2,64,128]{4,3,2,1,0:T(8,128)(2,1)S(1)}, bf16[2,2,2,64,128]{4,3,2,1,0:T(8,128)(2,1)S(1)}, u32[]{:S(2)}, u32[]{:S(2)}) %collective-permute-start.3) | collective-permute-done | bytes 131104 | tf_op jit(solution)/shard_map/ppermute | solution.py:246
  20.6 0.0 collective-permute-done.2
  20.6 0.5 %collective-permute-done.4 = bf16[2,2,2,64,128]{4,3,2,1,0:T(8,128)(2,1)S(1)} collective-permute-done((bf16[2,2,2,64,128]{4,3,2,1,0:T(8,128)(2,1)S(1)}, bf16[2,2,2,64,128]{4,3,2,1,0:T(8,128)(2,1)S(1)}, u32[]{:S(2)}, u32[]{:S(2)}) %collective-permute-start.4) | collective-permute-done | bytes 131104 | tf_op jit(solution)/shard_map/ppermute | solution.py:246
  21.1 0.9 %pad_maximum_fusion.parts_ref = bf16[4,2,2,2,64,128]{5,4,3,2,1,0:T(8,128)(2,1)} fusion(bf16[1,2,2,2,64,128]{5,4,3,2,1,0:T(8,128)(2,1)S(1)} %bitcast.15, bf16[1,2,2,2,64,128]{5,4,3,2,1,0:T(8,128)(2,1)S(1)} %bitcast.13, bf16[1,2,2,2,64,128]{5,4,3,2,1,0:T(8,128)(2,1)S(1)} %bitcast.14, bf16[1,2,2,2,64,128]{5,4,3,2,1,0:T(8,128)(2,1)S(1)} %get-tuple-element.4), kind=kLoop, calls=%fused_computation | loop fusion | flops 786432 | bytes 1048576 | tf_op jit(solution)/shard_map/stack | solution.py:247
  22.0 0.7 %broadcast_in_dim.2.mask_ref = f32[32,128]{1,0:T(8,128)} broadcast(f32[32]{0:T(128)S(1)} %convert_element_type.3), dimensions={0} | broadcast | bytes 16512 | tf_op jit(solution)/shard_map/broadcast_in_dim | solution.py:257
  22.6 22.8 %shard_map.84 = (bf16[8,8,128]{2,1,0:T(8,128)(2,1)}, bf16[8,8,128]{2,1,0:T(8,128)(2,1)}, f32[2,128,640]{2,1,0:T(8,128)}, f32[2,128,128]{2,1,0:T(8,128)}) custom-call(bf16[4,2,2,2,64,128]{5,4,3,2,1,0:T(8,128)(2,1)} %pad_maximum_fusion.parts_ref, f32[32,128]{1,0:T(8,128)} %broadcast_in_dim.2.mask_ref, bf16[2,128,640]{2,1,0:T(8,128)(2,1)} %w_in_ref.1, ...), custom_call_target="tpu_custom_call" | custom-call | tf_op jit(solution)/shard_map/pallas_call | solution.py:263
  (3 shorter events, 0.0 us)
Async XLA Ops:
  1.4 1.3 %collective-permute-start = (bf16[2,64,128]{2,1,0:T(8,128)(2,1)S(1)}, bf16[2,64,128]{2,1,0:T(8,128)(2,1)S(1)}, u32[]{:S(2)}, u32[]{:S(2)}) collective-permute-start(bf16[2,64,128]{2,1,0:T(8,128)(2,1)S(1)} %get-tuple-element.9), channel_id=1, source_target_pairs={{0,1},{1,0},{2,3},{3,2},{4,5},{5,4},{6,7},{7,6},{8,9},{9,8},{10,11... | collective-permute-start | bytes 98312 | tf_op jit(solution)/shard_map/ppermute | solution.py:246
  2.7 5.3 %collective-permute-start.1 = (bf16[2,2,64,128]{3,2,1,0:T(8,128)(2,1)S(1)}, bf16[2,2,64,128]{3,2,1,0:T(8,128)(2,1)S(1)}, u32[]{:S(2)}, u32[]{:S(2)}) collective-permute-start(bf16[2,2,64,128]{3,2,1,0:T(8,128)(2,1)S(1)} %get-tuple-element.7), channel_id=1, source_target_pairs={{0,2},{2,0},{1,3},{3,1},{4,6},{6,4},{5,7},{7,5},{8,10},{10,8},{9,1... | collective-permute-start | bytes 196616 | tf_op jit(solution)/shard_map/ppermute | solution.py:246
  8.0 6.8 %copy-start = (s32[32]{0:T(128)S(1)}, s32[32]{0:T(128)}, u32[]{:S(2)}) copy-start(s32[32]{0:T(128)} %param.7) | copy-start | bytes 388
  8.1 12.5 %collective-permute-start.3 = (bf16[2,2,2,64,128]{4,3,2,1,0:T(8,128)(2,1)S(1)}, bf16[2,2,2,64,128]{4,3,2,1,0:T(8,128)(2,1)S(1)}, u32[]{:S(2)}, u32[]{:S(2)}) collective-permute-start(bf16[2,2,2,64,128]{4,3,2,1,0:T(8,128)(2,1)S(1)} %get-tuple-element.5), channel_id=1, source_target_pairs={{0,8},{4,12},{8,0},{12,4},{1,9},{5,13},{9,1},{13,5},{2,10},{6,14},... | collective-permute-start | bytes 393224 | tf_op jit(solution)/shard_map/ppermute | solution.py:246
  11.1 9.5 %collective-permute-start.2 = (bf16[2,2,2,64,128]{4,3,2,1,0:T(8,128)(2,1)S(1)}, bf16[2,2,2,64,128]{4,3,2,1,0:T(8,128)(2,1)S(1)}, u32[]{:S(2)}, u32[]{:S(2)}) collective-permute-start(bf16[2,2,2,64,128]{4,3,2,1,0:T(8,128)(2,1)S(1)} %get-tuple-element.5), channel_id=1, source_target_pairs={{0,4},{4,8},{8,12},{12,0},{1,5},{5,9},{9,13},{13,1},{2,6},{6,10},{... | collective-permute-start | bytes 393224 | tf_op jit(solution)/shard_map/ppermute | solution.py:246
  12.6 8.5 %collective-permute-start.4 = (bf16[2,2,2,64,128]{4,3,2,1,0:T(8,128)(2,1)S(1)}, bf16[2,2,2,64,128]{4,3,2,1,0:T(8,128)(2,1)S(1)}, u32[]{:S(2)}, u32[]{:S(2)}) collective-permute-start(bf16[2,2,2,64,128]{4,3,2,1,0:T(8,128)(2,1)S(1)} %get-tuple-element.5), channel_id=1, source_target_pairs={{0,12},{4,0},{8,4},{12,8},{1,13},{5,1},{9,5},{13,9},{2,14},{6,2},{... | collective-permute-start | bytes 393224 | tf_op jit(solution)/shard_map/ppermute | solution.py:246

commit v2 on v0

--- a/solution.py
+++ b/solution.py
@@ -1,9 +1,319 @@
+import functools
+
 import jax
 import jax.numpy as jnp
 from jax import lax
+from jax.experimental import pallas as pl
+from jax.experimental.pallas import tpu as pltpu
 from jax.sharding import PartitionSpec as P
 
 EPSILON = 1e-05
+F32 = jnp.float32
+BF16 = jnp.bfloat16
+TILE = 8
+PLANES = 40
+FRONT = (1024, 1)
+MIDDLE = (1024, 1)
+TURN = (1024, 1)
+DOWN = (1024, 1)
+LAST = (1024, 1)
+TRI_GROUP = 16
+TRI_UNROLL = 2
+VMEM_BYTES = 40 * 2**20
+VMEM_PLAN = 40 * 2**20
+
+
+def dot(left, right):
+    return lax.dot_general(left, right, (((1,), (0,)), ((), ())), preferred_element_type=F32)
+
+
+def dot_rows(left, right):
+    return lax.dot_general(left, right, (((0,), (0,)), ((), ())), preferred_element_type=F32)
+
+
+def dot_last(left, right):
+    return lax.dot_general(left, right, (((1,), (1,)), ((), ())), preferred_element_type=F32)
+
+
+def lane_mean(values):
+    return jnp.mean(values, axis=-1, keepdims=True)
+
+
+def norm_of(values):
+    shifted = values - lane_mean(values)
+    inverse = lax.rsqrt(lane_mean(shifted * shifted) + EPSILON)
+    return shifted * inverse, inverse
+
+
+def norm_back(upstream, normed, inverse):
+    return inverse * (upstream - lane_mean(upstream) - normed * lane_mean(upstream * normed))
+
+
+def rounded(values):
+    return values.astype(BF16).astype(F32)
+
+
+def unrounded(values):
+    return values
+
+
+KEEP_TRI = rounded
+KEEP_STATE = rounded
+KEEP_GRAD = rounded
+KEEP_SIDE = rounded
+KEEP_GTRI = rounded
+
+
+def triangle(tokens, left, left_row, right, right_turned, target):
+    tiles = tokens // TILE
+
+    def right_tile(r, q):
+        if right_turned:
+            return right[pl.ds(q * TILE * tokens + r, TILE, stride=tokens), :]
+        return right[pl.ds(r * tokens + q * TILE, TILE), :]
+
+    def body(step, carry):
+        first = step * TRI_GROUP
+        totals = [[None] * tiles for _ in range(TRI_GROUP)]
+        for r in range(tokens):
+            column = [right_tile(r, q) for q in range(tiles)]
+            for p in range(TRI_GROUP):
+                scale = jnp.broadcast_to(left[pl.ds(left_row(first + p, r), 1), :], column[0].shape)
+                for q in range(tiles):
+                    term = scale * column[q]
+                    totals[p][q] = term if r == 0 else totals[p][q] + term
+        for p in range(TRI_GROUP):
+            for q in range(tiles):
+                at = pl.multiple_of((first + p) * tokens + q * TILE, TILE)
+                target[pl.ds(at, TILE), :] = totals[p][q]
+        return carry
+
+    lax.fori_loop(0, tokens // TRI_GROUP, body, 0, unroll=TRI_UNROLL)
+
+
+def whole_kernel(
+    tokens, sizes, refs_in, mask_ref, w_in_ref, w_out_ref,
+    updated_ref, pair_grad_ref, gwi_ref, gwo_ref,
+    states, cot, flat, side, normed, inv, normed16, one_a, two_a, one_b, two_b,
+    gate, tnorm, tinv, tnorm16, slope, tri, ga, gb,
+    w_half, w_turned, wo_turned, gproj, gh, mask,
+):
+    n_row, n_chan, n_sub = sizes
+    row_id, chan_id, sub_id = lax.axis_index("row"), lax.axis_index("chan"), lax.axis_index("sub")
+    rows, cols = tokens // n_row, tokens // (n_chan * n_sub)
+    pairs = tokens * tokens
+    hidden = w_out_ref.shape[1]
+    channels = w_in_ref.shape[1]
+    gy_ref = cot
+
+    place(tokens, sizes, refs_in, states.at[0], gy_ref)
+
+    for u in range(2):
+        w_turned[u] = w_in_ref[u].T
+        wo_turned[u] = w_out_ref[u].T
+        for k in range(5):
+            at = slice(hidden * k, hidden * (k + 1))
+            values = w_in_ref[u, :, at]
+            w_half[u, :, at] = values * jnp.asarray(0.5, BF16) if k in (1, 3, 4) else values
+    for j in range(tokens):
+        mask[j : j + 1, :] = jnp.full((1, channels), mask_ref[j].astype(F32))
+
+    def half_mask(step, chunk):
+        lines = chunk // tokens
+        outer = mask[pl.ds(step * lines, lines), :] * 0.5
+        return (outer[:, None, :] * mask[...][None, :, :]).reshape(chunk, channels)
+
+    def at_chunk(step, chunk):
+        return pl.ds(pl.multiple_of(step * chunk, chunk), chunk)
+
+    def front(u, x, step, chunk):
+        here = at_chunk(step, chunk)
+        n, s = norm_of(x)
+        normed[u, here, :] = n
+        inv[u, here, :] = jnp.broadcast_to(s, n.shape)
+        n16 = n.astype(BF16)
+        normed16[u, here, :] = n16
+        projected = dot(n16, w_half[u])
+        pa, qa, pb, qb, qz = [projected[:, hidden * k : hidden * (k + 1)] for k in range(5)]
+        half = half_mask(step, chunk)
+        for p, q, one, two, keep in ((pa, qa, one_a, two_a, flat), (pb, qb, one_b, two_b, side)):
+            first = half * jnp.tanh(q) + half
+            value = first * p
+            one[u, here, :] = first
+            two[u, here, :] = value - value * first
+            keep[u, here, :] = KEEP_SIDE(value)
+        gate[u, here, :] = 0.5 * jnp.tanh(qz) + 0.5
+
+    def back(u, step, chunk):
+        here = at_chunk(step, chunk)
+        tn, r = norm_of(KEEP_TRI(tri[here, :]))
+        tnorm[u, here, :] = tn
+        tinv[u, here, :] = jnp.broadcast_to(r, tn.shape)
+        tn16 = tn.astype(BF16)
+        tnorm16[u, here, :] = tn16
+        z = gate[u, here, :]
+        gated = z * dot(tn16, w_out_ref[u])
+        slope[u, here, :] = gated - gated * z
+        return KEEP_STATE(states[u, here, :] + gated)
+
+    def grad_back(u, gy, step, chunk):
+        here = at_chunk(step, chunk)
+        gh16 = (gy * gate[u, here, :]).astype(BF16)
+        gh[here, :] = gh16
+        gtri = norm_back(dot(gh16, wo_turned[u]), tnorm[u, here, :], tinv[u, here, :])
+        tri[here, :] = KEEP_GTRI(gtri)
+
+    def grad_front(u, gy, step, chunk):
+        here = at_chunk(step, chunk)
+        ga_here, gb_here = KEEP_GRAD(ga[here, :]), KEEP_GRAD(gb[here, :])
+        pieces = [
+            ga_here * one_a[u, here, :],
+            ga_here * two_a[u, here, :],
+            gb_here * one_b[u, here, :],
+            gb_here * two_b[u, here, :],
+            gy * slope[u, here, :],
+        ]
+        for k, piece in enumerate(pieces):
+            gproj[here, hidden * k : hidden * (k + 1)] = piece.astype(BF16)
+
+    def grad_state(u, gy, here):
+        h = dot(gproj[here, :], w_turned[u])
+        return gy + norm_back(h, normed[u, here, :], inv[u, here, :])
+
+    def loop(body, chunk, unroll):
+        def step_of(step, carry):
+            body(step, chunk)
+            return carry
+
+        lax.fori_loop(0, pairs // chunk, step_of, 0, unroll=unroll)
+
+    natural = lambda p, r: p * tokens + r
+    turned = lambda p, r: r * tokens + p
+
+    loop(lambda step, chunk: front(0, states[0, at_chunk(step, chunk), :], step, chunk), *FRONT)
+    triangle(tokens, flat.at[0], natural, side.at[0], True, tri)
+
+    def middle(step, chunk):
+        x1 = back(0, step, chunk)
+        states[1, at_chunk(step, chunk), :] = x1
+        front(1, x1, step, chunk)
+
+    loop(middle, *MIDDLE)
+    triangle(tokens, flat.at[1], turned, side.at[1], False, tri)
+
+    def turn(step, chunk):
+        here = at_chunk(step, chunk)
+        states[0, here, :] = back(1, step, chunk)
+        grad_back(1, gy_ref[here, :], step, chunk)
+
+    loop(turn, *TURN)
+    gwo_ref[1] = dot_rows(tnorm16[1], gh[...]) * (1.0 / tokens)
+
+    triangle(tokens, side.at[1], natural, tri, True, ga)
+    triangle(tokens, flat.at[1], natural, tri, False, gb)
+
+    def down(step, chunk):
+        here = at_chunk(step, chunk)
+        grad_front(1, gy_ref[here, :], step, chunk)
+        gx = grad_state(1, gy_ref[here, :], here)
+        gy_ref[here, :] = gx
+        grad_back(0, gx, step, chunk)
+
+    loop(down, *DOWN)
+    gwi_ref[1] = dot_rows(normed16[1], gproj[...]) * (1.0 / tokens)
+    gwo_ref[0] = dot_rows(tnorm16[0], gh[...]) * (1.0 / tokens)
+
+    triangle(tokens, tri, natural, side.at[0], False, ga)
+    triangle(tokens, tri, turned, flat.at[0], False, gb)
+
+    def last(step, chunk):
+        grad_front(0, gy_ref[at_chunk(step, chunk), :], step, chunk)
+
+    loop(last, *LAST)
+    own = rows * tokens
+    here = pl.ds(pl.multiple_of(row_id * own, own), own)
+    gy_ref[here, :] = grad_state(0, gy_ref[here, :], here)
+    gwi_ref[0] = dot_rows(normed16[0], gproj[...]) * (1.0 / tokens)
+
+    c0 = pl.multiple_of((chan_id * n_sub + sub_id) * cols, TILE)
+    for source, target in ((states.at[0], updated_ref), (gy_ref, pair_grad_ref)):
+        for r in range(rows):
+            at = pl.multiple_of((row_id * rows + r) * tokens + c0, TILE)
+            target[r] = source[pl.ds(at, cols), :].astype(BF16)
+
+
+def place(tokens, sizes, refs_in, x_ref, gy_ref):
+    n_row, n_chan, n_sub = sizes
+    row_id, chan_id, sub_id = lax.axis_index("row"), lax.axis_index("chan"), lax.axis_index("sub")
+    rows, cols = tokens // n_row, tokens // (n_chan * n_sub)
+    channels = x_ref.shape[-1]
+    for place_in_list, ref in enumerate(refs_in):
+        chan_step, sub_step = place_in_list // n_sub, place_in_list % n_sub
+        chan, sub = jnp.bitwise_xor(chan_id, chan_step), jnp.bitwise_xor(sub_id, sub_step)
+        c0 = (chan * n_sub + sub) * cols
+        for row_step in range(n_row):
+            row = jnp.bitwise_xor(row_id, row_step)
+            for kind, target in ((0, x_ref), (1, gy_ref)):
+                block = ref[row_step, kind].astype(F32).reshape(rows, cols, channels)
+                for r in range(rows):
+                    at = pl.multiple_of((row * rows + r) * tokens + c0, TILE)
+                    target[pl.ds(at, cols), :] = block[r]
+
+
+def from_step(block, axis, size, step):
+    return lax.ppermute(block, axis, [(i, i ^ step) for i in range(size)])
+
+
+def gather_part(pair, cotangent, sizes):
+    n_row, n_chan, n_sub = sizes
+    channels = pair.shape[-1]
+    mine = jnp.stack([pair.reshape(-1, channels), cotangent.reshape(-1, channels)])
+    far = {step: from_step(mine, "row", n_row, step) for step in range(n_row - 1, 0, -1)}
+    column = jnp.stack([mine] + [far[step] for step in range(1, n_row)])
+    parts = []
+    for chan_step in range(n_chan):
+        near = column if chan_step == 0 else from_step(column, "chan", n_chan, chan_step)
+        parts += [near if step == 0 else from_step(near, "sub", n_sub, step) for step in range(n_sub)]
+    return parts
+
+
+def whole_part(sizes, pair, cotangent, token_mask, w_in, w_out):
+    tokens = token_mask.shape[0]
+    channels = pair.shape[-1]
+    hidden = w_out.shape[1]
+    pairs = tokens * tokens
+    parts = gather_part(pair, cotangent, sizes)
+    plane = pltpu.VMEM((pairs, channels), F32)
+    two = pltpu.VMEM((2, pairs, channels), F32)
+    two16 = pltpu.VMEM((2, pairs, channels), BF16)
+    vmem = pl.BlockSpec(memory_space=pltpu.VMEM)
+
+    def kernel(*refs):
+        count = len(parts)
+        whole_kernel(tokens, sizes, refs[:count], *refs[count:])
+
+    return pl.pallas_call(
+        kernel,
+        out_shape=(
+            jax.ShapeDtypeStruct(pair.shape, BF16),
+            jax.ShapeDtypeStruct(pair.shape, BF16),
+            jax.ShapeDtypeStruct(w_in.shape, F32),
+            jax.ShapeDtypeStruct(w_out.shape, F32),
+        ),
+        in_specs=[vmem] * len(parts) + [pl.BlockSpec(memory_space=pltpu.SMEM), vmem, vmem],
+        out_specs=(vmem,) * 4,
+        scratch_shapes=[
+            two, plane, two, two, two, two, two16, two, two, two, two,
+            two, two, two, two16, two, plane, plane, plane,
+            pltpu.VMEM(w_in.shape, BF16),
+            pltpu.VMEM((2, w_in.shape[2], channels), BF16),
+            pltpu.VMEM((2, channels, hidden), BF16),
+            pltpu.VMEM((pairs, w_in.shape[2]), BF16),
+            pltpu.VMEM((pairs, channels), BF16),
+            pltpu.VMEM((tokens, channels), F32),
+        ],
+        compiler_params=pltpu.CompilerParams(vmem_limit_bytes=VMEM_BYTES),
+    )(*parts, token_mask, w_in, w_out)
 
 
 def layer_norm(values, norm_axis):
@@ -117,7 +427,7 @@
     return folder(initial, lax.all_gather(source, "row", axis=1, tiled=True), jnp.int32(0))
 
 
-def shards(pair, cotangent, token_mask, w_in, w_out):
+def spread_part(pair, cotangent, token_mask, w_in, w_out):
     row_count, col_count, _ = pair.shape
     hidden = w_out.shape[1]
     token_total = token_mask.shape[0]
@@ -201,6 +511,16 @@
 
 
 def solution(mesh):
+    sizes = tuple(mesh.shape[axis] for axis in ("row", "chan", "sub"))
+
+    def shards(pair, cotangent, token_mask, w_in, w_out):
+        tokens = token_mask.shape[0]
+        tiled = tokens % (TILE * sizes[1] * sizes[2]) == 0
+        tiled = tiled and all(size & (size - 1) == 0 for size in sizes)
+        if tiled and PLANES * tokens * tokens * pair.shape[-1] * 4 <= VMEM_PLAN:
+            return whole_part(sizes, pair, cotangent, token_mask, w_in, w_out)
+        return spread_part(pair, cotangent, token_mask, w_in, w_out)
+
     placed = (
         P(("groups", "row"), ("chan", "sub"), None),
         P(("groups", "row"), ("chan", "sub"), None),

time: 253 us -> 34.2 us (0.14)
  waiting for transfers between devices: 112 us -> 10.5 us
  blocking collectives: 67.3 us -> 0 us
  starting transfers between devices: 26.1 us -> 7.18 us
  local copies, waits for them, and re-layouts: 19.2 us -> 0.85 us
  between operations: 14.8 us -> 0.65 us
  Pallas kernels: 0 us -> 13.9 us
  other arithmetic: 7.05 us -> 0.81 us
  matrix products: 5.95 us -> 0 us
    psum x1 -> x0, waiting for transfers between devices: 89 us -> none  [shards(): lax.psum((jnp.stack(wi_grads), jnp.stack(wo_grads)), ('row', 'chan', 'sub'))]
    all_gather x4 -> x0, blocking collectives: 53.2 us -> none  [fold_rows(): lax.all_gather(source, 'row', axis=1, tiled=True)]
    all_to_all x8 -> x0, starting transfers between devices: 26.1 us -> none  [the longest x3 9.78 us: to_columns(): lax.all_to_all(stacked, ('chan', 'sub'), split_axis=3, concat_axis=1, til...]
    all_to_all x8 -> x0, waiting for transfers between devices: 22.5 us -> none  [the longest x3 10.3 us: to_columns(): lax.all_to_all(stacked, ('chan', 'sub'), split_axis=3, concat_axis=1, til...]
    all_to_all x2 -> x0, blocking collectives: 14.2 us -> none  [the longest x1 7.95 us: to_channels(): lax.all_to_all(stacked, ('chan', 'sub'), split_axis=1, concat_axis=3, til...]
    pallas_call x0 -> x1, Pallas kernels: none -> 13.9 us  [whole_part(): pl.pallas_call(kernel, out_shape=(jax.ShapeDtypeStruct(pair.shape, BF16),...]
    unnamed x31 -> x6, local copies, waits for them, and re-layouts: 11.8 us -> 0.85 us
    ppermute x0 -> x6, waiting for transfers between devices: none -> 10.5 us  [from_step(): return lax.ppermute(block, axis, [(i, i ^ step) for i in range(size)])]
  transfers between devices with their start and end apart: 9 -> 6, of which waited for: 7 -> 5; matrix products, arithmetic and copies ran while one was open for 1% -> 0% of each run, Pallas kernels for 0% -> 0%
where the time goes in v2:
time: 34.2 us; the launch traced here: 33.9 us
  Pallas kernels  13.9 us (41%)
  waiting for transfers between devices  10.5 us (31%)
  starting transfers between devices  7.18 us (21%)
  local copies, waits for them, and re-layouts  0.85 us (2%)
  other arithmetic  0.81 us (2%)
  between operations  0.65 us (2%)
    pallas_call x1, Pallas kernels, whole_part(): pl.pallas_call(kernel, out_shape=(jax.ShapeDtypeStruct(pair.shape, BF16),...  13.9 us
    ppermute x6, waiting for transfers between devices, from_step(): return lax.ppermute(block, axis, [(i, i ^ step) for i in range(size)])  10.5 us
    ppermute x6, starting transfers between devices, from_step(): return lax.ppermute(block, axis, [(i, i ^ step) for i in range(size)])  7.18 us
    unnamed x6, local copies, waits for them, and re-layouts  0.85 us
    another operation x2, other arithmetic, gather_part(): column = jnp.stack([mine] + [far[step] for step in range(1, n_row)])  0.81 us
  transfers between devices with their start and end apart: 6, of which 5 were waited for; matrix products, arithmetic and copies ran while one was open for 0% of the time, Pallas kernels for 0%

profile of v2, /device:TPU:0, one launch (start us, length us, event | category | flops | bytes accessed | tf_op | source)
XLA Modules:
  0.0 33.9 jit_solution(13667087122744414094)
XLA Ops:
  0.6 0.0 copy-start
  0.6 0.8 %fusion = (bf16[1,2,64,128]{3,2,1,0:T(8,128)(2,1)S(1)}, bf16[2,64,128]{2,1,0:T(8,128)(2,1)S(1)}) fusion(bf16[1,64,128]{2,1,0:T(8,128)(2,1)} %bitcast.10, bf16[1,64,128]{2,1,0:T(8,128)(2,1)} %bitcast.11), kind=kLoop, calls=%fused_computation.2 | loop fusion | flops 16384 | bytes 98304 | tf_op jit(solution)/shard_map/stack | solution.py:272
  1.4 4.0 %collective-permute-start.1 = (bf16[2,64,128]{2,1,0:T(8,128)(2,1)S(1)}, bf16[2,64,128]{2,1,0:T(8,128)(2,1)S(1)}, u32[]{:S(2)}, u32[]{:S(2)}) collective-permute-start(bf16[2,64,128]{2,1,0:T(8,128)(2,1)S(1)} %get-tuple-element.5), channel_id=1, source_target_pairs={{0,8},{4,12},{8,0},{12,4},{1,9},{5,13},{9,1},{13,5},{2,10},{6,14},... | collective-permute-start | bytes 98312 | tf_op jit(solution)/shard_map/ppermute | solution.py:264
  5.5 1.6 %collective-permute-start = (bf16[2,64,128]{2,1,0:T(8,128)(2,1)S(1)}, bf16[2,64,128]{2,1,0:T(8,128)(2,1)S(1)}, u32[]{:S(2)}, u32[]{:S(2)}) collective-permute-start(bf16[2,64,128]{2,1,0:T(8,128)(2,1)S(1)} %get-tuple-element.5), channel_id=1, source_target_pairs={{0,4},{4,0},{8,12},{12,8},{1,5},{5,1},{9,13},{13,9},{2,6},{6,2},{1... | collective-permute-start | bytes 98312 | tf_op jit(solution)/shard_map/ppermute | solution.py:264
  7.0 0.0 collective-permute-start.2
  7.0 0.8 %collective-permute-done.1 = bf16[2,64,128]{2,1,0:T(8,128)(2,1)S(1)} collective-permute-done((bf16[2,64,128]{2,1,0:T(8,128)(2,1)S(1)}, bf16[2,64,128]{2,1,0:T(8,128)(2,1)S(1)}, u32[]{:S(2)}, u32[]{:S(2)}) %collective-permute-start.1) | collective-permute-done | bytes 32800 | tf_op jit(solution)/shard_map/ppermute | solution.py:264
  7.8 1.6 %collective-permute-done = bf16[2,64,128]{2,1,0:T(8,128)(2,1)S(1)} collective-permute-done((bf16[2,64,128]{2,1,0:T(8,128)(2,1)S(1)}, bf16[2,64,128]{2,1,0:T(8,128)(2,1)S(1)}, u32[]{:S(2)}, u32[]{:S(2)}) %collective-permute-start) | collective-permute-done | bytes 32800 | tf_op jit(solution)/shard_map/ppermute | solution.py:264
  9.4 3.4 %collective-permute-done.2 = bf16[2,64,128]{2,1,0:T(8,128)(2,1)S(1)} collective-permute-done((bf16[2,64,128]{2,1,0:T(8,128)(2,1)S(1)}, bf16[2,64,128]{2,1,0:T(8,128)(2,1)S(1)}, u32[]{:S(2)}, u32[]{:S(2)}) %collective-permute-start.2) | collective-permute-done | bytes 32800 | tf_op jit(solution)/shard_map/ppermute | solution.py:264
  12.8 0.0 copy-start.2
  12.8 1.6 %collective-permute-start.4 = (bf16[4,2,64,128]{3,2,1,0:T(8,128)(2,1)S(1)}, bf16[4,2,64,128]{3,2,1,0:T(8,128)(2,1)S(1)}, u32[]{:S(2)}, u32[]{:S(2)}) collective-permute-start(bf16[4,2,64,128]{3,2,1,0:T(8,128)(2,1)S(1)} %pad_maximum_fusion.refs_0_), channel_id=1, source_target_pairs={{0,2},{2,0},{1,3},{3,1},{4,6},{6,4},{5,7},{7,5},{8,10},{10,8},{9,1... | collective-permute-start | bytes 393224 | tf_op jit(solution)/shard_map/ppermute | solution.py:264
  14.3 0.0 collective-permute-start.3
  14.3 3.5 %collective-permute-done.4.refs_2_ = bf16[4,2,64,128]{3,2,1,0:T(8,128)(2,1)S(1)} collective-permute-done((bf16[4,2,64,128]{3,2,1,0:T(8,128)(2,1)S(1)}, bf16[4,2,64,128]{3,2,1,0:T(8,128)(2,1)S(1)}, u32[]{:S(2)}, u32[]{:S(2)}) %collective-permute-start.4) | collective-permute-done | bytes 131104 | tf_op jit(solution)/shard_map/ppermute | solution.py:264
  17.8 0.0 collective-permute-start.5
  17.8 0.0 collective-permute-done.3.refs_1_
  17.8 1.3 %collective-permute-done.5.refs_3_ = bf16[4,2,64,128]{3,2,1,0:T(8,128)(2,1)S(1)} collective-permute-done((bf16[4,2,64,128]{3,2,1,0:T(8,128)(2,1)S(1)}, bf16[4,2,64,128]{3,2,1,0:T(8,128)(2,1)S(1)}, u32[]{:S(2)}, u32[]{:S(2)}) %collective-permute-start.5) | collective-permute-done | bytes 131104 | tf_op jit(solution)/shard_map/ppermute | solution.py:264
  19.2 0.0 copy-done
  19.2 0.0 copy-done.2
  19.2 0.0 copy-start.1
  19.2 0.8 %copy-done.1 = bf16[2,128,128]{2,1,0:T(8,128)(2,1)S(1)} copy-done((bf16[2,128,128]{2,1,0:T(8,128)(2,1)S(1)}, bf16[2,128,128]{2,1,0:T(8,128)(2,1)}, u32[]{:S(2)}) %copy-start.1) | copy-done | bytes 65560
  20.0 13.9 %shard_map.84 = (bf16[8,8,128]{2,1,0:T(8,128)(2,1)}, bf16[8,8,128]{2,1,0:T(8,128)(2,1)}, f32[2,128,640]{2,1,0:T(8,128)}, f32[2,128,128]{2,1,0:T(8,128)}) custom-call(bf16[4,2,64,128]{3,2,1,0:T(8,128)(2,1)S(1)} %pad_maximum_fusion.refs_0_, bf16[4,2,64,128]{3,2,1,0:T(8,128)(2,1)S(1)} %collective-permute-done.3.refs_1_, ...), custom_call_target="tpu_custom_call" | custom-call | tf_op jit(solution)/shard_map/pallas_call | solution.py:295
  (1 shorter events, 0.0 us)
Async XLA Ops:
  0.6 18.5 %copy-start = (bf16[2,128,640]{2,1,0:T(8,128)(2,1)S(1)}, bf16[2,128,640]{2,1,0:T(8,128)(2,1)}, u32[]{:S(2)}) copy-start(bf16[2,128,640]{2,1,0:T(8,128)(2,1)} %refs_5_.1) | copy-start | bytes 983044
  1.4 6.4 %collective-permute-start.1 = (bf16[2,64,128]{2,1,0:T(8,128)(2,1)S(1)}, bf16[2,64,128]{2,1,0:T(8,128)(2,1)S(1)}, u32[]{:S(2)}, u32[]{:S(2)}) collective-permute-start(bf16[2,64,128]{2,1,0:T(8,128)(2,1)S(1)} %get-tuple-element.5), channel_id=1, source_target_pairs={{0,8},{4,12},{8,0},{12,4},{1,9},{5,13},{9,1},{13,5},{2,10},{6,14},... | collective-permute-start | bytes 98312 | tf_op jit(solution)/shard_map/ppermute | solution.py:264
  5.5 3.9 %collective-permute-start = (bf16[2,64,128]{2,1,0:T(8,128)(2,1)S(1)}, bf16[2,64,128]{2,1,0:T(8,128)(2,1)S(1)}, u32[]{:S(2)}, u32[]{:S(2)}) collective-permute-start(bf16[2,64,128]{2,1,0:T(8,128)(2,1)S(1)} %get-tuple-element.5), channel_id=1, source_target_pairs={{0,4},{4,0},{8,12},{12,8},{1,5},{5,1},{9,13},{13,9},{2,6},{6,2},{1... | collective-permute-start | bytes 98312 | tf_op jit(solution)/shard_map/ppermute | solution.py:264
  7.0 5.7 %collective-permute-start.2 = (bf16[2,64,128]{2,1,0:T(8,128)(2,1)S(1)}, bf16[2,64,128]{2,1,0:T(8,128)(2,1)S(1)}, u32[]{:S(2)}, u32[]{:S(2)}) collective-permute-start(bf16[2,64,128]{2,1,0:T(8,128)(2,1)S(1)} %get-tuple-element.5), channel_id=1, source_target_pairs={{0,12},{4,8},{8,4},{12,0},{1,13},{5,9},{9,5},{13,1},{2,14},{6,10},... | collective-permute-start | bytes 98312 | tf_op jit(solution)/shard_map/ppermute | solution.py:264
  12.8 6.4 %copy-start.2 = (s32[32]{0:T(128)S(1)}, s32[32]{0:T(128)}, u32[]{:S(2)}) copy-start(s32[32]{0:T(128)} %refs_4_.1) | copy-start | bytes 388
  12.8 5.0 %collective-permute-start.4 = (bf16[4,2,64,128]{3,2,1,0:T(8,128)(2,1)S(1)}, bf16[4,2,64,128]{3,2,1,0:T(8,128)(2,1)S(1)}, u32[]{:S(2)}, u32[]{:S(2)}) collective-permute-start(bf16[4,2,64,128]{3,2,1,0:T(8,128)(2,1)S(1)} %pad_maximum_fusion.refs_0_), channel_id=1, source_target_pairs={{0,2},{2,0},{1,3},{3,1},{4,6},{6,4},{5,7},{7,5},{8,10},{10,8},{9,1... | collective-permute-start | bytes 393224 | tf_op jit(solution)/shard_map/ppermute | solution.py:264
  14.3 3.5 %collective-permute-start.3 = (bf16[4,2,64,128]{3,2,1,0:T(8,128)(2,1)S(1)}, bf16[4,2,64,128]{3,2,1,0:T(8,128)(2,1)S(1)}, u32[]{:S(2)}, u32[]{:S(2)}) collective-permute-start(bf16[4,2,64,128]{3,2,1,0:T(8,128)(2,1)S(1)} %pad_maximum_fusion.refs_0_), channel_id=1, source_target_pairs={{0,1},{1,0},{2,3},{3,2},{4,5},{5,4},{6,7},{7,6},{8,9},{9,8},{10,11... | collective-permute-start | bytes 393224 | tf_op jit(solution)/shard_map/ppermute | solution.py:264
  17.8 1.3 %collective-permute-start.5 = (bf16[4,2,64,128]{3,2,1,0:T(8,128)(2,1)S(1)}, bf16[4,2,64,128]{3,2,1,0:T(8,128)(2,1)S(1)}, u32[]{:S(2)}, u32[]{:S(2)}) collective-permute-start(bf16[4,2,64,128]{3,2,1,0:T(8,128)(2,1)S(1)} %collective-permute-done.4.refs_2_), channel_id=1, source_target_pairs={{0,1},{1,0},{2,3},{3,2},{4,5},{5,4},{6,7},{7,6},{8,9},{9,8},{10,11... | collective-permute-start | bytes 393224 | tf_op jit(solution)/shard_map/ppermute | solution.py:264
  19.2 0.8 %copy-start.1 = (bf16[2,128,128]{2,1,0:T(8,128)(2,1)S(1)}, bf16[2,128,128]{2,1,0:T(8,128)(2,1)}, u32[]{:S(2)}) copy-start(bf16[2,128,128]{2,1,0:T(8,128)(2,1)} %refs_6_.1) | copy-start | bytes 196612

commit v3 on v2

--- a/solution.py
+++ b/solution.py
@@ -11,6 +11,7 @@
 F32 = jnp.float32
 BF16 = jnp.bfloat16
 TILE = 8
+X_PARTS = 2
 PLANES = 40
 FRONT = (1024, 1)
 MIDDLE = (1024, 1)
@@ -19,7 +20,7 @@
 LAST = (1024, 1)
 TRI_GROUP = 16
 TRI_UNROLL = 2
-VMEM_BYTES = 40 * 2**20
+VMEM_BYTES = 28 * 2**20
 VMEM_PLAN = 40 * 2**20
 
 
@@ -92,11 +93,11 @@
 
 
 def whole_kernel(
-    tokens, sizes, refs_in, mask_ref, w_in_ref, w_out_ref,
+    tokens, sizes, pieces, refs_in, mask_hbm, w_in_hbm, w_out_hbm,
     updated_ref, pair_grad_ref, gwi_ref, gwo_ref,
     states, cot, flat, side, normed, inv, normed16, one_a, two_a, one_b, two_b,
     gate, tnorm, tinv, tnorm16, slope, tri, ga, gb,
-    w_half, w_turned, wo_turned, gproj, gh, mask,
+    w_half, w_turned, wo_turned, gproj, gh, mask, mask_ref, w_in_ref, w_out_ref, sem,
 ):
     n_row, n_chan, n_sub = sizes
     row_id, chan_id, sub_id = lax.axis_index("row"), lax.axis_index("chan"), lax.axis_index("sub")
@@ -106,7 +107,15 @@
     channels = w_in_ref.shape[1]
     gy_ref = cot
 
-    place(tokens, sizes, refs_in, states.at[0], gy_ref)
+    copies = [
+        pltpu.make_async_copy(source, target, sem.at[k])
+        for k, (source, target) in enumerate(((mask_hbm, mask_ref), (w_in_hbm, w_in_ref), (w_out_hbm, w_out_ref)))
+    ]
+    for copy in copies:
+        copy.start()
+    place(tokens, sizes, pieces, refs_in, states.at[0], gy_ref)
+    for copy in copies:
+        copy.wait()
 
     for u in range(2):
         w_turned[u] = w_in_ref[u].T
@@ -242,19 +251,18 @@
             target[r] = source[pl.ds(at, cols), :].astype(BF16)
 
 
-def place(tokens, sizes, refs_in, x_ref, gy_ref):
+def place(tokens, sizes, pieces, refs_in, x_ref, gy_ref):
     n_row, n_chan, n_sub = sizes
     row_id, chan_id, sub_id = lax.axis_index("row"), lax.axis_index("chan"), lax.axis_index("sub")
     rows, cols = tokens // n_row, tokens // (n_chan * n_sub)
     channels = x_ref.shape[-1]
-    for place_in_list, ref in enumerate(refs_in):
-        chan_step, sub_step = place_in_list // n_sub, place_in_list % n_sub
+    for ref, (row_steps, chan_step, sub_step) in zip(refs_in, pieces):
         chan, sub = jnp.bitwise_xor(chan_id, chan_step), jnp.bitwise_xor(sub_id, sub_step)
         c0 = (chan * n_sub + sub) * cols
-        for row_step in range(n_row):
+        for k, row_step in enumerate(row_steps):
             row = jnp.bitwise_xor(row_id, row_step)
             for kind, target in ((0, x_ref), (1, gy_ref)):
-                block = ref[row_step, kind].astype(F32).reshape(rows, cols, channels)
+                block = ref[k, kind].astype(F32).reshape(rows, cols, channels)
                 for r in range(rows):
                     at = pl.multiple_of((row * rows + r) * tokens + c0, TILE)
                     target[pl.ds(at, cols), :] = block[r]
@@ -268,13 +276,20 @@
     n_row, n_chan, n_sub = sizes
     channels = pair.shape[-1]
     mine = jnp.stack([pair.reshape(-1, channels), cotangent.reshape(-1, channels)])
-    far = {step: from_step(mine, "row", n_row, step) for step in range(n_row - 1, 0, -1)}
-    column = jnp.stack([mine] + [far[step] for step in range(1, n_row)])
-    parts = []
-    for chan_step in range(n_chan):
-        near = column if chan_step == 0 else from_step(column, "chan", n_chan, chan_step)
-        parts += [near if step == 0 else from_step(near, "sub", n_sub, step) for step in range(n_sub)]
-    return parts
+    row_steps = [0] + list(range(n_row - 1, 0, -1))
+    column = jnp.stack([mine] + [from_step(mine, "row", n_row, step) for step in row_steps[1:]])
+    parts = [column]
+    pieces = [(row_steps, 0, 0)]
+    cut = max(n_row // X_PARTS, 1)
+    for chan_step in range(1, n_chan):
+        for first in range(0, n_row, cut):
+            parts.append(from_step(column[first : first + cut], "chan", n_chan, chan_step))
+            pieces.append((row_steps[first : first + cut], chan_step, 0))
+    for part, (steps, chan_step, _) in list(zip(parts, pieces)):
+        for sub_step in range(1, n_sub):
+            parts.append(from_step(part, "sub", n_sub, sub_step))
+            pieces.append((steps, chan_step, sub_step))
+    return parts, pieces
 
 
 def whole_part(sizes, pair, cotangent, token_mask, w_in, w_out):
@@ -282,7 +297,7 @@
     channels = pair.shape[-1]
     hidden = w_out.shape[1]
     pairs = tokens * tokens
-    parts = gather_part(pair, cotangent, sizes)
+    parts, pieces = gather_part(pair, cotangent, sizes)
     plane = pltpu.VMEM((pairs, channels), F32)
     two = pltpu.VMEM((2, pairs, channels), F32)
     two16 = pltpu.VMEM((2, pairs, channels), BF16)
@@ -290,7 +305,7 @@
 
     def kernel(*refs):
         count = len(parts)
-        whole_kernel(tokens, sizes, refs[:count], *refs[count:])
+        whole_kernel(tokens, sizes, pieces, refs[:count], *refs[count:])
 
     return pl.pallas_call(
         kernel,
@@ -300,7 +315,7 @@
             jax.ShapeDtypeStruct(w_in.shape, F32),
             jax.ShapeDtypeStruct(w_out.shape, F32),
         ),
-        in_specs=[vmem] * len(parts) + [pl.BlockSpec(memory_space=pltpu.SMEM), vmem, vmem],
+        in_specs=[vmem] * len(parts) + [pl.BlockSpec(memory_space=pltpu.HBM)] * 3,
         out_specs=(vmem,) * 4,
         scratch_shapes=[
             two, plane, two, two, two, two, two16, two, two, two, two,
@@ -311,6 +326,10 @@
             pltpu.VMEM((pairs, w_in.shape[2]), BF16),
             pltpu.VMEM((pairs, channels), BF16),
             pltpu.VMEM((tokens, channels), F32),
+            pltpu.SMEM((tokens,), jnp.int32),
+            pltpu.VMEM(w_in.shape, BF16),
+            pltpu.VMEM(w_out.shape, BF16),
+            pltpu.SemaphoreType.DMA((3,)),
         ],
         compiler_params=pltpu.CompilerParams(vmem_limit_bytes=VMEM_BYTES),
     )(*parts, token_mask, w_in, w_out)

time: 34.2 us -> 30.9 us (0.904)
  waiting for transfers between devices: 10.5 us -> 5.87 us
  starting transfers between devices: 7.18 us -> 9.54 us
  local copies, waits for them, and re-layouts: 0.85 us -> 0.02 us
    ppermute x6 -> x8, waiting for transfers between devices: 10.5 us -> 5.87 us  [from_step(): return lax.ppermute(block, axis, [(i, i ^ step) for i in range(size)])]
    ppermute x6 -> x8, starting transfers between devices: 7.18 us -> 9.54 us  [from_step(): return lax.ppermute(block, axis, [(i, i ^ step) for i in range(size)])]
    unnamed x6, local copies, waits for them, and re-layouts: 0.85 us -> 0.02 us
    another operation x2 -> x4, other arithmetic: 0.81 us -> 0.82 us  [gather_part(): jnp.stack([mine] + [from_step(mine, 'row', n_row, step) for step in row_s...]
  transfers between devices with their start and end apart: 6 -> 8, of which waited for: 5 -> 5; matrix products, arithmetic and copies ran while one was open for 0% -> 0% of each run, Pallas kernels for 0% -> 0%
where the time goes in v3:
time: 30.9 us; the launch traced here: 30.7 us
  Pallas kernels  13.7 us (44%)
  starting transfers between devices  9.54 us (31%)
  waiting for transfers between devices  5.87 us (19%)
  other arithmetic  0.82 us (3%)
  between operations  0.69 us (2%)
    pallas_call x1, Pallas kernels, whole_part(): pl.pallas_call(kernel, out_shape=(jax.ShapeDtypeStruct(pair.shape, BF16),...  13.7 us
    ppermute x8, starting transfers between devices, from_step(): return lax.ppermute(block, axis, [(i, i ^ step) for i in range(size)])  9.54 us
    ppermute x8, waiting for transfers between devices, from_step(): return lax.ppermute(block, axis, [(i, i ^ step) for i in range(size)])  5.87 us
    another operation x4, other arithmetic, gather_part(): jnp.stack([mine] + [from_step(mine, 'row', n_row, step) for step in row_s...  0.82 us
  transfers between devices with their start and end apart: 8, of which 5 were waited for; matrix products, arithmetic and copies ran while one was open for 0% of the time, Pallas kernels for 0%

profile of v3, /device:TPU:0, one launch (start us, length us, event | category | flops | bytes accessed | tf_op | source)
XLA Modules:
  0.0 30.7 jit_solution(7285406407200521099)
XLA Ops:
  0.6 0.0 copy-start
  0.6 0.8 %fusion = (bf16[1,2,64,128]{3,2,1,0:T(8,128)(2,1)S(1)}, bf16[2,64,128]{2,1,0:T(8,128)(2,1)S(1)}) fusion(bf16[1,64,128]{2,1,0:T(8,128)(2,1)} %bitcast.13, bf16[1,64,128]{2,1,0:T(8,128)(2,1)} %bitcast.14), kind=kLoop, calls=%fused_computation.4 | loop fusion | flops 16384 | bytes 98304 | tf_op jit(solution)/shard_map/stack | solution.py:280
  1.4 5.0 %collective-permute-start = (bf16[2,64,128]{2,1,0:T(8,128)(2,1)S(1)}, bf16[2,64,128]{2,1,0:T(8,128)(2,1)S(1)}, u32[]{:S(2)}, u32[]{:S(2)}) collective-permute-start(bf16[2,64,128]{2,1,0:T(8,128)(2,1)S(1)} %get-tuple-element.5), channel_id=1, source_target_pairs={{0,12},{4,8},{8,4},{12,0},{1,13},{5,9},{9,5},{13,1},{2,14},{6,10},... | collective-permute-start | bytes 98312 | tf_op jit(solution)/shard_map/ppermute | solution.py:272
  6.5 0.0 collective-permute-start.1
  6.5 0.6 %collective-permute-start.2 = (bf16[2,64,128]{2,1,0:T(8,128)(2,1)S(1)}, bf16[2,64,128]{2,1,0:T(8,128)(2,1)S(1)}, u32[]{:S(2)}, u32[]{:S(2)}) collective-permute-start(bf16[2,64,128]{2,1,0:T(8,128)(2,1)S(1)} %get-tuple-element.5), channel_id=1, source_target_pairs={{0,4},{4,0},{8,12},{12,8},{1,5},{5,1},{9,13},{13,9},{2,6},{6,2},{1... | collective-permute-start | bytes 98312 | tf_op jit(solution)/shard_map/ppermute | solution.py:272
  7.1 1.3 %collective-permute-done = bf16[2,64,128]{2,1,0:T(8,128)(2,1)S(1)} collective-permute-done((bf16[2,64,128]{2,1,0:T(8,128)(2,1)S(1)}, bf16[2,64,128]{2,1,0:T(8,128)(2,1)S(1)}, u32[]{:S(2)}, u32[]{:S(2)}) %collective-permute-start) | collective-permute-done | bytes 32800 | tf_op jit(solution)/shard_map/ppermute | solution.py:272
  8.4 1.8 %collective-permute-start.3 = (bf16[2,2,64,128]{3,2,1,0:T(8,128)(2,1)S(1)}, bf16[2,2,64,128]{3,2,1,0:T(8,128)(2,1)S(1)}, u32[]{:S(2)}, u32[]{:S(2)}) collective-permute-start(bf16[2,2,64,128]{3,2,1,0:T(8,128)(2,1)S(1)} %pad_maximum_fusion.1), channel_id=1, source_target_pairs={{0,2},{2,0},{1,3},{3,1},{4,6},{6,4},{5,7},{7,5},{8,10},{10,8},{9,1... | collective-permute-start | bytes 196616 | tf_op jit(solution)/shard_map/ppermute | solution.py:272
  10.2 1.1 %collective-permute-done.1 = bf16[2,64,128]{2,1,0:T(8,128)(2,1)S(1)} collective-permute-done((bf16[2,64,128]{2,1,0:T(8,128)(2,1)S(1)}, bf16[2,64,128]{2,1,0:T(8,128)(2,1)S(1)}, u32[]{:S(2)}, u32[]{:S(2)}) %collective-permute-start.1) | collective-permute-done | bytes 32800 | tf_op jit(solution)/shard_map/ppermute | solution.py:272
  11.3 0.0 collective-permute-done.2
  11.3 0.0 copy-start.1
  11.3 0.0 copy-start.2
  11.3 1.6 %collective-permute-start.4 = (bf16[2,2,64,128]{3,2,1,0:T(8,128)(2,1)S(1)}, bf16[2,2,64,128]{3,2,1,0:T(8,128)(2,1)S(1)}, u32[]{:S(2)}, u32[]{:S(2)}) collective-permute-start(bf16[2,2,64,128]{3,2,1,0:T(8,128)(2,1)S(1)} %pad_maximum_fusion.2), channel_id=1, source_target_pairs={{0,2},{2,0},{1,3},{3,1},{4,6},{6,4},{5,7},{7,5},{8,10},{10,8},{9,1... | collective-permute-start | bytes 196616 | tf_op jit(solution)/shard_map/ppermute | solution.py:272
  12.9 0.1 collective-permute-start.5
  13.0 0.1 collective-permute-done.3.refs_1_
  13.1 0.4 %collective-permute-start.6 = (bf16[2,2,64,128]{3,2,1,0:T(8,128)(2,1)S(1)}, bf16[2,2,64,128]{3,2,1,0:T(8,128)(2,1)S(1)}, u32[]{:S(2)}, u32[]{:S(2)}) collective-permute-start(bf16[2,2,64,128]{3,2,1,0:T(8,128)(2,1)S(1)} %collective-permute-done.3.refs_1_), channel_id=1, source_target_pairs={{0,1},{1,0},{2,3},{3,2},{4,5},{5,4},{6,7},{7,6},{8,9},{9,8},{10,11... | collective-permute-start | bytes 196616 | tf_op jit(solution)/shard_map/ppermute | solution.py:272
  13.5 2.2 %collective-permute-done.4.refs_2_ = bf16[2,2,64,128]{3,2,1,0:T(8,128)(2,1)S(1)} collective-permute-done((bf16[2,2,64,128]{3,2,1,0:T(8,128)(2,1)S(1)}, bf16[2,2,64,128]{3,2,1,0:T(8,128)(2,1)S(1)}, u32[]{:S(2)}, u32[]{:S(2)}) %collective-permute-start.4) | collective-permute-done | bytes 65568 | tf_op jit(solution)/shard_map/ppermute | solution.py:272
  15.7 0.0 collective-permute-start.7
  15.7 0.0 collective-permute-done.6.refs_4_
  15.7 1.2 %collective-permute-done.7.refs_5_ = bf16[2,2,64,128]{3,2,1,0:T(8,128)(2,1)S(1)} collective-permute-done((bf16[2,2,64,128]{3,2,1,0:T(8,128)(2,1)S(1)}, bf16[2,2,64,128]{3,2,1,0:T(8,128)(2,1)S(1)}, u32[]{:S(2)}, u32[]{:S(2)}) %collective-permute-start.7) | collective-permute-done | bytes 65568 | tf_op jit(solution)/shard_map/ppermute | solution.py:272
  16.9 0.0 collective-permute-done.5.refs_3_
  16.9 0.0 copy-done
  16.9 0.0 copy-done.1
  16.9 0.0 copy-done.2
  16.9 13.7 %shard_map.84 = (bf16[8,8,128]{2,1,0:T(8,128)(2,1)}, bf16[8,8,128]{2,1,0:T(8,128)(2,1)}, f32[2,128,640]{2,1,0:T(8,128)}, f32[2,128,128]{2,1,0:T(8,128)}) custom-call(bf16[4,2,64,128]{3,2,1,0:T(8,128)(2,1)S(1)} %pad_maximum_fusion.refs_0_, bf16[2,2,64,128]{3,2,1,0:T(8,128)(2,1)S(1)} %collective-permute-done.3.refs_1_, ...), custom_call_target="tpu_custom_call" | custom-call | tf_op jit(solution)/shard_map/pallas_call | solution.py:310
  (3 shorter events, 0.0 us)
Async XLA Ops:
  0.6 16.3 %copy-start = (bf16[2,128,640]{2,1,0:T(8,128)(2,1)S(1)}, bf16[2,128,640]{2,1,0:T(8,128)(2,1)}, u32[]{:S(2)}) copy-start(bf16[2,128,640]{2,1,0:T(8,128)(2,1)} %refs_7_.1) | copy-start | bytes 983044
  1.4 6.9 %collective-permute-start = (bf16[2,64,128]{2,1,0:T(8,128)(2,1)S(1)}, bf16[2,64,128]{2,1,0:T(8,128)(2,1)S(1)}, u32[]{:S(2)}, u32[]{:S(2)}) collective-permute-start(bf16[2,64,128]{2,1,0:T(8,128)(2,1)S(1)} %get-tuple-element.5), channel_id=1, source_target_pairs={{0,12},{4,8},{8,4},{12,0},{1,13},{5,9},{9,5},{13,1},{2,14},{6,10},... | collective-permute-start | bytes 98312 | tf_op jit(solution)/shard_map/ppermute | solution.py:272
  6.5 4.8 %collective-permute-start.1 = (bf16[2,64,128]{2,1,0:T(8,128)(2,1)S(1)}, bf16[2,64,128]{2,1,0:T(8,128)(2,1)S(1)}, u32[]{:S(2)}, u32[]{:S(2)}) collective-permute-start(bf16[2,64,128]{2,1,0:T(8,128)(2,1)S(1)} %get-tuple-element.5), channel_id=1, source_target_pairs={{0,8},{4,12},{8,0},{12,4},{1,9},{5,13},{9,1},{13,5},{2,10},{6,14},... | collective-permute-start | bytes 98312 | tf_op jit(solution)/shard_map/ppermute | solution.py:272
  6.5 4.8 %collective-permute-start.2 = (bf16[2,64,128]{2,1,0:T(8,128)(2,1)S(1)}, bf16[2,64,128]{2,1,0:T(8,128)(2,1)S(1)}, u32[]{:S(2)}, u32[]{:S(2)}) collective-permute-start(bf16[2,64,128]{2,1,0:T(8,128)(2,1)S(1)} %get-tuple-element.5), channel_id=1, source_target_pairs={{0,4},{4,0},{8,12},{12,8},{1,5},{5,1},{9,13},{13,9},{2,6},{6,2},{1... | collective-permute-start | bytes 98312 | tf_op jit(solution)/shard_map/ppermute | solution.py:272
  8.4 4.7 %collective-permute-start.3 = (bf16[2,2,64,128]{3,2,1,0:T(8,128)(2,1)S(1)}, bf16[2,2,64,128]{3,2,1,0:T(8,128)(2,1)S(1)}, u32[]{:S(2)}, u32[]{:S(2)}) collective-permute-start(bf16[2,2,64,128]{3,2,1,0:T(8,128)(2,1)S(1)} %pad_maximum_fusion.1), channel_id=1, source_target_pairs={{0,2},{2,0},{1,3},{3,1},{4,6},{6,4},{5,7},{7,5},{8,10},{10,8},{9,1... | collective-permute-start | bytes 196616 | tf_op jit(solution)/shard_map/ppermute | solution.py:272
  11.3 5.6 %copy-start.1 = (bf16[2,128,128]{2,1,0:T(8,128)(2,1)S(1)}, bf16[2,128,128]{2,1,0:T(8,128)(2,1)}, u32[]{:S(2)}) copy-start(bf16[2,128,128]{2,1,0:T(8,128)(2,1)} %refs_8_.1) | copy-start | bytes 196612
  11.3 5.6 %copy-start.2 = (s32[32]{0:T(128)S(1)}, s32[32]{0:T(128)}, u32[]{:S(2)}) copy-start(s32[32]{0:T(128)} %refs_6_.1) | copy-start | bytes 388
  11.3 4.3 %collective-permute-start.4 = (bf16[2,2,64,128]{3,2,1,0:T(8,128)(2,1)S(1)}, bf16[2,2,64,128]{3,2,1,0:T(8,128)(2,1)S(1)}, u32[]{:S(2)}, u32[]{:S(2)}) collective-permute-start(bf16[2,2,64,128]{3,2,1,0:T(8,128)(2,1)S(1)} %pad_maximum_fusion.2), channel_id=1, source_target_pairs={{0,2},{2,0},{1,3},{3,1},{4,6},{6,4},{5,7},{7,5},{8,10},{10,8},{9,1... | collective-permute-start | bytes 196616 | tf_op jit(solution)/shard_map/ppermute | solution.py:272
  12.9 4.0 %collective-permute-start.5 = (bf16[4,2,64,128]{3,2,1,0:T(8,128)(2,1)S(1)}, bf16[4,2,64,128]{3,2,1,0:T(8,128)(2,1)S(1)}, u32[]{:S(2)}, u32[]{:S(2)}) collective-permute-start(bf16[4,2,64,128]{3,2,1,0:T(8,128)(2,1)S(1)} %pad_maximum_fusion.refs_0_), channel_id=1, source_target_pairs={{0,1},{1,0},{2,3},{3,2},{4,5},{5,4},{6,7},{7,6},{8,9},{9,8},{10,11... | collective-permute-start | bytes 393224 | tf_op jit(solution)/shard_map/ppermute | solution.py:272
  13.1 2.6 %collective-permute-start.6 = (bf16[2,2,64,128]{3,2,1,0:T(8,128)(2,1)S(1)}, bf16[2,2,64,128]{3,2,1,0:T(8,128)(2,1)S(1)}, u32[]{:S(2)}, u32[]{:S(2)}) collective-permute-start(bf16[2,2,64,128]{3,2,1,0:T(8,128)(2,1)S(1)} %collective-permute-done.3.refs_1_), channel_id=1, source_target_pairs={{0,1},{1,0},{2,3},{3,2},{4,5},{5,4},{6,7},{7,6},{8,9},{9,8},{10,11... | collective-permute-start | bytes 196616 | tf_op jit(solution)/shard_map/ppermute | solution.py:272
  15.7 1.3 %collective-permute-start.7 = (bf16[2,2,64,128]{3,2,1,0:T(8,128)(2,1)S(1)}, bf16[2,2,64,128]{3,2,1,0:T(8,128)(2,1)S(1)}, u32[]{:S(2)}, u32[]{:S(2)}) collective-permute-start(bf16[2,2,64,128]{3,2,1,0:T(8,128)(2,1)S(1)} %collective-permute-done.4.refs_2_), channel_id=1, source_target_pairs={{0,1},{1,0},{2,3},{3,2},{4,5},{5,4},{6,7},{7,6},{8,9},{9,8},{10,11... | collective-permute-start | bytes 196616 | tf_op jit(solution)/shard_map/ppermute | solution.py:272

commit v4 on v3

--- a/solution.py
+++ b/solution.py
@@ -12,14 +12,16 @@
 BF16 = jnp.bfloat16
 TILE = 8
 X_PARTS = 2
+TILE16 = 16
+SUM = 8
 PLANES = 40
 FRONT = (1024, 1)
 MIDDLE = (1024, 1)
 TURN = (1024, 1)
 DOWN = (1024, 1)
 LAST = (1024, 1)
-TRI_GROUP = 16
-TRI_UNROLL = 2
+TRI_GROUP = 8
+TRI_UNROLL = 4
 VMEM_BYTES = 28 * 2**20
 VMEM_PLAN = 40 * 2**20
 
@@ -40,8 +42,9 @@
     return jnp.mean(values, axis=-1, keepdims=True)
 
 
-def norm_of(values):
-    shifted = values - lane_mean(values)
+def norm_of(values16):
+    channels = values16.shape[-1]
+    shifted = values16.astype(F32) - dot(values16, jnp.full((channels, channels), 1.0 / channels, BF16))
     inverse = lax.rsqrt(lane_mean(shifted * shifted) + EPSILON)
     return shifted * inverse, inverse
 
@@ -61,32 +64,36 @@
 KEEP_TRI = rounded
 KEEP_STATE = rounded
 KEEP_GRAD = rounded
-KEEP_SIDE = rounded
-KEEP_GTRI = rounded
-
-
-def triangle(tokens, left, left_row, right, right_turned, target):
-    tiles = tokens // TILE
-
-    def right_tile(r, q):
-        if right_turned:
-            return right[pl.ds(q * TILE * tokens + r, TILE, stride=tokens), :]
-        return right[pl.ds(r * tokens + q * TILE, TILE), :]
+
+
+def triangle(tokens, left, left_row, right16, target):
+    channels = target.shape[-1]
+    tiles = tokens // TILE16
 
     def body(step, carry):
         first = step * TRI_GROUP
         totals = [[None] * tiles for _ in range(TRI_GROUP)]
-        for r in range(tokens):
-            column = [right_tile(r, q) for q in range(tiles)]
+        for g in range(0, tokens, SUM):
+            terms = [[[] for _ in range(tiles)] for _ in range(TRI_GROUP)]
+            for r in range(g, g + SUM):
+                column = [right16[pl.ds(r * tokens + q * TILE16, TILE16), :] for q in range(tiles)]
+                for p in range(TRI_GROUP):
+                    scale = left[pl.ds(left_row(first + p, r), 1), :]
+                    scale = jnp.broadcast_to(scale, (TILE16, channels)).astype(BF16)
+                    for q in range(tiles):
+                        level = terms[p][q]
+                        level.append((scale * column[q], 1))
+                        while len(level) > 1 and level[-1][1] == level[-2][1]:
+                            (last, size), (other, _) = level.pop(), level.pop()
+                            level.append((other + last, 2 * size))
             for p in range(TRI_GROUP):
-                scale = jnp.broadcast_to(left[pl.ds(left_row(first + p, r), 1), :], column[0].shape)
                 for q in range(tiles):
-                    term = scale * column[q]
-                    totals[p][q] = term if r == 0 else totals[p][q] + term
+                    value = terms[p][q][0][0].astype(F32)
+                    totals[p][q] = value if g == 0 else totals[p][q] + value
         for p in range(TRI_GROUP):
             for q in range(tiles):
-                at = pl.multiple_of((first + p) * tokens + q * TILE, TILE)
-                target[pl.ds(at, TILE), :] = totals[p][q]
+                at = pl.multiple_of((first + p) * tokens + q * TILE16, TILE16)
+                target[pl.ds(at, TILE16), :] = totals[p][q]
         return carry
 
     lax.fori_loop(0, tokens // TRI_GROUP, body, 0, unroll=TRI_UNROLL)
@@ -95,8 +102,8 @@
 def whole_kernel(
     tokens, sizes, pieces, refs_in, mask_hbm, w_in_hbm, w_out_hbm,
     updated_ref, pair_grad_ref, gwi_ref, gwo_ref,
-    states, cot, flat, side, normed, inv, normed16, one_a, two_a, one_b, two_b,
-    gate, tnorm, tinv, tnorm16, slope, tri, ga, gb,
+    states, cot, flat, side, flat16, side16, normed, inv, normed16, one_a, two_a, one_b, two_b,
+    gate, tnorm, tinv, tnorm16, slope, tri, tri16, turned16, ga, gb,
     w_half, w_turned, wo_turned, gproj, gh, mask, mask_ref, w_in_ref, w_out_ref, sem,
 ):
     n_row, n_chan, n_sub = sizes
@@ -135,9 +142,9 @@
     def at_chunk(step, chunk):
         return pl.ds(pl.multiple_of(step * chunk, chunk), chunk)
 
-    def front(u, x, step, chunk):
+    def front(u, x16, step, chunk):
         here = at_chunk(step, chunk)
-        n, s = norm_of(x)
+        n, s = norm_of(x16)
         normed[u, here, :] = n
         inv[u, here, :] = jnp.broadcast_to(s, n.shape)
         n16 = n.astype(BF16)
@@ -145,17 +152,21 @@
         projected = dot(n16, w_half[u])
         pa, qa, pb, qb, qz = [projected[:, hidden * k : hidden * (k + 1)] for k in range(5)]
         half = half_mask(step, chunk)
-        for p, q, one, two, keep in ((pa, qa, one_a, two_a, flat), (pb, qb, one_b, two_b, side)):
+        for p, q, one, two, keep, keep16 in (
+            (pa, qa, one_a, two_a, flat, flat16),
+            (pb, qb, one_b, two_b, side, side16),
+        ):
             first = half * jnp.tanh(q) + half
             value = first * p
             one[u, here, :] = first
             two[u, here, :] = value - value * first
-            keep[u, here, :] = KEEP_SIDE(value)
+            keep[u, here, :] = value
+            keep16[u, here, :] = value.astype(BF16)
         gate[u, here, :] = 0.5 * jnp.tanh(qz) + 0.5
 
     def back(u, step, chunk):
         here = at_chunk(step, chunk)
-        tn, r = norm_of(KEEP_TRI(tri[here, :]))
+        tn, r = norm_of(tri[here, :].astype(BF16))
         tnorm[u, here, :] = tn
         tinv[u, here, :] = jnp.broadcast_to(r, tn.shape)
         tn16 = tn.astype(BF16)
@@ -163,14 +174,16 @@
         z = gate[u, here, :]
         gated = z * dot(tn16, w_out_ref[u])
         slope[u, here, :] = gated - gated * z
-        return KEEP_STATE(states[u, here, :] + gated)
+        return (states[u, here, :] + gated).astype(BF16)
 
     def grad_back(u, gy, step, chunk):
         here = at_chunk(step, chunk)
         gh16 = (gy * gate[u, here, :]).astype(BF16)
         gh[here, :] = gh16
         gtri = norm_back(dot(gh16, wo_turned[u]), tnorm[u, here, :], tinv[u, here, :])
-        tri[here, :] = KEEP_GTRI(gtri)
+        tri[here, :] = gtri
+        if u == 1:
+            tri16[here, :] = gtri.astype(BF16)
 
     def grad_front(u, gy, step, chunk):
         here = at_chunk(step, chunk)
@@ -196,30 +209,41 @@
 
         lax.fori_loop(0, pairs // chunk, step_of, 0, unroll=unroll)
 
+    def turn_pairs(source):
+        for r in range(tokens):
+            for q in range(tokens // TILE16):
+                halves = [
+                    source[pl.ds((q * TILE16 + half) * tokens + r, TILE, stride=tokens), :] for half in (0, TILE)
+                ]
+                at = r * tokens + q * TILE16
+                turned16[at : at + TILE16, :] = jnp.concatenate(halves, axis=0).astype(BF16)
+
     natural = lambda p, r: p * tokens + r
     turned = lambda p, r: r * tokens + p
 
-    loop(lambda step, chunk: front(0, states[0, at_chunk(step, chunk), :], step, chunk), *FRONT)
-    triangle(tokens, flat.at[0], natural, side.at[0], True, tri)
+    loop(lambda step, chunk: front(0, states[0, at_chunk(step, chunk), :].astype(BF16), step, chunk), *FRONT)
+    turn_pairs(side.at[0])
+    triangle(tokens, flat.at[0], natural, turned16, tri)
 
     def middle(step, chunk):
         x1 = back(0, step, chunk)
-        states[1, at_chunk(step, chunk), :] = x1
+        states[1, at_chunk(step, chunk), :] = x1.astype(F32)
         front(1, x1, step, chunk)
 
     loop(middle, *MIDDLE)
-    triangle(tokens, flat.at[1], turned, side.at[1], False, tri)
+    triangle(tokens, flat.at[1], turned, side16.at[1], tri)
 
     def turn(step, chunk):
         here = at_chunk(step, chunk)
-        states[0, here, :] = back(1, step, chunk)
+        states[0, here, :] = back(1, step, chunk).astype(F32)
         grad_back(1, gy_ref[here, :], step, chunk)
 
     loop(turn, *TURN)
     gwo_ref[1] = dot_rows(tnorm16[1], gh[...]) * (1.0 / tokens)
 
-    triangle(tokens, side.at[1], natural, tri, True, ga)
-    triangle(tokens, flat.at[1], natural, tri, False, gb)
+    turn_pairs(tri)
+    triangle(tokens, side.at[1], natural, turned16, ga)
+    triangle(tokens, flat.at[1], natural, tri16, gb)
 
     def down(step, chunk):
         here = at_chunk(step, chunk)
@@ -232,8 +256,8 @@
     gwi_ref[1] = dot_rows(normed16[1], gproj[...]) * (1.0 / tokens)
     gwo_ref[0] = dot_rows(tnorm16[0], gh[...]) * (1.0 / tokens)
 
-    triangle(tokens, tri, natural, side.at[0], False, ga)
-    triangle(tokens, tri, turned, flat.at[0], False, gb)
+    triangle(tokens, tri, natural, side16.at[0], ga)
+    triangle(tokens, tri, turned, flat16.at[0], gb)
 
     def last(step, chunk):
         grad_front(0, gy_ref[at_chunk(step, chunk), :], step, chunk)
@@ -301,6 +325,7 @@
     plane = pltpu.VMEM((pairs, channels), F32)
     two = pltpu.VMEM((2, pairs, channels), F32)
     two16 = pltpu.VMEM((2, pairs, channels), BF16)
+    plane16 = pltpu.VMEM((pairs, channels), BF16)
     vmem = pl.BlockSpec(memory_space=pltpu.VMEM)
 
     def kernel(*refs):
@@ -318,8 +343,8 @@
         in_specs=[vmem] * len(parts) + [pl.BlockSpec(memory_space=pltpu.HBM)] * 3,
         out_specs=(vmem,) * 4,
         scratch_shapes=[
-            two, plane, two, two, two, two, two16, two, two, two, two,
-            two, two, two, two16, two, plane, plane, plane,
+            two, plane, two, two, two16, two16, two, two, two16, two, two, two, two,
+            two, two, two, two16, two, plane, plane16, plane16, plane, plane,
             pltpu.VMEM(w_in.shape, BF16),
             pltpu.VMEM((2, w_in.shape[2], channels), BF16),
             pltpu.VMEM((2, channels, hidden), BF16),

time: 30.9 us -> 28.4 us (0.919)
  Pallas kernels: 13.7 us -> 11.2 us
    pallas_call x1, Pallas kernels: 13.7 us -> 11.2 us  [whole_part(): pl.pallas_call(kernel, out_shape=(jax.ShapeDtypeStruct(pair.shape, BF16),...]
where the time goes in v4:
time: 28.4 us; the launch traced here: 28.1 us
  Pallas kernels  11.2 us (39%)
  starting transfers between devices  9.54 us (34%)
  waiting for transfers between devices  5.87 us (21%)
  other arithmetic  0.82 us (3%)
  between operations  0.69 us (2%)
    pallas_call x1, Pallas kernels, whole_part(): pl.pallas_call(kernel, out_shape=(jax.ShapeDtypeStruct(pair.shape, BF16),...  11.2 us
    ppermute x8, starting transfers between devices, from_step(): return lax.ppermute(block, axis, [(i, i ^ step) for i in range(size)])  9.54 us
    ppermute x8, waiting for transfers between devices, from_step(): return lax.ppermute(block, axis, [(i, i ^ step) for i in range(size)])  5.87 us
    another operation x4, other arithmetic, gather_part(): jnp.stack([mine] + [from_step(mine, 'row', n_row, step) for step in row_s...  0.82 us
  transfers between devices with their start and end apart: 8, of which 5 were waited for; matrix products, arithmetic and copies ran while one was open for 0% of the time, Pallas kernels for 0%

profile of v4, /device:TPU:0, one launch (start us, length us, event | category | flops | bytes accessed | tf_op | source)
XLA Modules:
  0.0 28.1 jit_solution(8598317159838134845)
XLA Ops:
  0.6 0.0 copy-start
  0.6 0.8 %fusion = (bf16[1,2,64,128]{3,2,1,0:T(8,128)(2,1)S(1)}, bf16[2,64,128]{2,1,0:T(8,128)(2,1)S(1)}) fusion(bf16[1,64,128]{2,1,0:T(8,128)(2,1)} %bitcast.13, bf16[1,64,128]{2,1,0:T(8,128)(2,1)} %bitcast.14), kind=kLoop, calls=%fused_computation.4 | loop fusion | flops 16384 | bytes 98304 | tf_op jit(solution)/shard_map/stack | solution.py:304
  1.4 5.0 %collective-permute-start = (bf16[2,64,128]{2,1,0:T(8,128)(2,1)S(1)}, bf16[2,64,128]{2,1,0:T(8,128)(2,1)S(1)}, u32[]{:S(2)}, u32[]{:S(2)}) collective-permute-start(bf16[2,64,128]{2,1,0:T(8,128)(2,1)S(1)} %get-tuple-element.5), channel_id=1, source_target_pairs={{0,12},{4,8},{8,4},{12,0},{1,13},{5,9},{9,5},{13,1},{2,14},{6,10},... | collective-permute-start | bytes 98312 | tf_op jit(solution)/shard_map/ppermute | solution.py:296
  6.5 0.0 collective-permute-start.1
  6.5 0.6 %collective-permute-start.2 = (bf16[2,64,128]{2,1,0:T(8,128)(2,1)S(1)}, bf16[2,64,128]{2,1,0:T(8,128)(2,1)S(1)}, u32[]{:S(2)}, u32[]{:S(2)}) collective-permute-start(bf16[2,64,128]{2,1,0:T(8,128)(2,1)S(1)} %get-tuple-element.5), channel_id=1, source_target_pairs={{0,4},{4,0},{8,12},{12,8},{1,5},{5,1},{9,13},{13,9},{2,6},{6,2},{1... | collective-permute-start | bytes 98312 | tf_op jit(solution)/shard_map/ppermute | solution.py:296
  7.1 1.3 %collective-permute-done = bf16[2,64,128]{2,1,0:T(8,128)(2,1)S(1)} collective-permute-done((bf16[2,64,128]{2,1,0:T(8,128)(2,1)S(1)}, bf16[2,64,128]{2,1,0:T(8,128)(2,1)S(1)}, u32[]{:S(2)}, u32[]{:S(2)}) %collective-permute-start) | collective-permute-done | bytes 32800 | tf_op jit(solution)/shard_map/ppermute | solution.py:296
  8.4 1.8 %collective-permute-start.3 = (bf16[2,2,64,128]{3,2,1,0:T(8,128)(2,1)S(1)}, bf16[2,2,64,128]{3,2,1,0:T(8,128)(2,1)S(1)}, u32[]{:S(2)}, u32[]{:S(2)}) collective-permute-start(bf16[2,2,64,128]{3,2,1,0:T(8,128)(2,1)S(1)} %pad_maximum_fusion.1), channel_id=1, source_target_pairs={{0,2},{2,0},{1,3},{3,1},{4,6},{6,4},{5,7},{7,5},{8,10},{10,8},{9,1... | collective-permute-start | bytes 196616 | tf_op jit(solution)/shard_map/ppermute | solution.py:296
  10.2 1.1 %collective-permute-done.1 = bf16[2,64,128]{2,1,0:T(8,128)(2,1)S(1)} collective-permute-done((bf16[2,64,128]{2,1,0:T(8,128)(2,1)S(1)}, bf16[2,64,128]{2,1,0:T(8,128)(2,1)S(1)}, u32[]{:S(2)}, u32[]{:S(2)}) %collective-permute-start.1) | collective-permute-done | bytes 32800 | tf_op jit(solution)/shard_map/ppermute | solution.py:296
  11.3 0.0 collective-permute-done.2
  11.3 0.0 copy-start.1
  11.3 0.0 copy-start.2
  11.3 1.6 %collective-permute-start.4 = (bf16[2,2,64,128]{3,2,1,0:T(8,128)(2,1)S(1)}, bf16[2,2,64,128]{3,2,1,0:T(8,128)(2,1)S(1)}, u32[]{:S(2)}, u32[]{:S(2)}) collective-permute-start(bf16[2,2,64,128]{3,2,1,0:T(8,128)(2,1)S(1)} %pad_maximum_fusion.2), channel_id=1, source_target_pairs={{0,2},{2,0},{1,3},{3,1},{4,6},{6,4},{5,7},{7,5},{8,10},{10,8},{9,1... | collective-permute-start | bytes 196616 | tf_op jit(solution)/shard_map/ppermute | solution.py:296
  12.9 0.1 collective-permute-start.5
  13.0 0.1 collective-permute-done.3.refs_1_
  13.1 0.4 %collective-permute-start.6 = (bf16[2,2,64,128]{3,2,1,0:T(8,128)(2,1)S(1)}, bf16[2,2,64,128]{3,2,1,0:T(8,128)(2,1)S(1)}, u32[]{:S(2)}, u32[]{:S(2)}) collective-permute-start(bf16[2,2,64,128]{3,2,1,0:T(8,128)(2,1)S(1)} %collective-permute-done.3.refs_1_), channel_id=1, source_target_pairs={{0,1},{1,0},{2,3},{3,2},{4,5},{5,4},{6,7},{7,6},{8,9},{9,8},{10,11... | collective-permute-start | bytes 196616 | tf_op jit(solution)/shard_map/ppermute | solution.py:296
  13.5 2.2 %collective-permute-done.4.refs_2_ = bf16[2,2,64,128]{3,2,1,0:T(8,128)(2,1)S(1)} collective-permute-done((bf16[2,2,64,128]{3,2,1,0:T(8,128)(2,1)S(1)}, bf16[2,2,64,128]{3,2,1,0:T(8,128)(2,1)S(1)}, u32[]{:S(2)}, u32[]{:S(2)}) %collective-permute-start.4) | collective-permute-done | bytes 65568 | tf_op jit(solution)/shard_map/ppermute | solution.py:296
  15.7 0.0 collective-permute-start.7
  15.7 0.0 collective-permute-done.6.refs_4_
  15.7 1.2 %collective-permute-done.7.refs_5_ = bf16[2,2,64,128]{3,2,1,0:T(8,128)(2,1)S(1)} collective-permute-done((bf16[2,2,64,128]{3,2,1,0:T(8,128)(2,1)S(1)}, bf16[2,2,64,128]{3,2,1,0:T(8,128)(2,1)S(1)}, u32[]{:S(2)}, u32[]{:S(2)}) %collective-permute-start.7) | collective-permute-done | bytes 65568 | tf_op jit(solution)/shard_map/ppermute | solution.py:296
  16.9 0.0 collective-permute-done.5.refs_3_
  16.9 0.0 copy-done
  16.9 0.0 copy-done.1
  16.9 0.0 copy-done.2
  16.9 11.2 %shard_map.84 = (bf16[8,8,128]{2,1,0:T(8,128)(2,1)}, bf16[8,8,128]{2,1,0:T(8,128)(2,1)}, f32[2,128,640]{2,1,0:T(8,128)}, f32[2,128,128]{2,1,0:T(8,128)}) custom-call(bf16[4,2,64,128]{3,2,1,0:T(8,128)(2,1)S(1)} %pad_maximum_fusion.refs_0_, bf16[2,2,64,128]{3,2,1,0:T(8,128)(2,1)S(1)} %collective-permute-done.3.refs_1_, ...), custom_call_target="tpu_custom_call" | custom-call | tf_op jit(solution)/shard_map/pallas_call | solution.py:335
  (3 shorter events, 0.0 us)
Async XLA Ops:
  0.6 16.3 %copy-start = (bf16[2,128,640]{2,1,0:T(8,128)(2,1)S(1)}, bf16[2,128,640]{2,1,0:T(8,128)(2,1)}, u32[]{:S(2)}) copy-start(bf16[2,128,640]{2,1,0:T(8,128)(2,1)} %refs_7_.1) | copy-start | bytes 983044
  1.4 6.9 %collective-permute-start = (bf16[2,64,128]{2,1,0:T(8,128)(2,1)S(1)}, bf16[2,64,128]{2,1,0:T(8,128)(2,1)S(1)}, u32[]{:S(2)}, u32[]{:S(2)}) collective-permute-start(bf16[2,64,128]{2,1,0:T(8,128)(2,1)S(1)} %get-tuple-element.5), channel_id=1, source_target_pairs={{0,12},{4,8},{8,4},{12,0},{1,13},{5,9},{9,5},{13,1},{2,14},{6,10},... | collective-permute-start | bytes 98312 | tf_op jit(solution)/shard_map/ppermute | solution.py:296
  6.5 4.8 %collective-permute-start.1 = (bf16[2,64,128]{2,1,0:T(8,128)(2,1)S(1)}, bf16[2,64,128]{2,1,0:T(8,128)(2,1)S(1)}, u32[]{:S(2)}, u32[]{:S(2)}) collective-permute-start(bf16[2,64,128]{2,1,0:T(8,128)(2,1)S(1)} %get-tuple-element.5), channel_id=1, source_target_pairs={{0,8},{4,12},{8,0},{12,4},{1,9},{5,13},{9,1},{13,5},{2,10},{6,14},... | collective-permute-start | bytes 98312 | tf_op jit(solution)/shard_map/ppermute | solution.py:296
  6.5 4.8 %collective-permute-start.2 = (bf16[2,64,128]{2,1,0:T(8,128)(2,1)S(1)}, bf16[2,64,128]{2,1,0:T(8,128)(2,1)S(1)}, u32[]{:S(2)}, u32[]{:S(2)}) collective-permute-start(bf16[2,64,128]{2,1,0:T(8,128)(2,1)S(1)} %get-tuple-element.5), channel_id=1, source_target_pairs={{0,4},{4,0},{8,12},{12,8},{1,5},{5,1},{9,13},{13,9},{2,6},{6,2},{1... | collective-permute-start | bytes 98312 | tf_op jit(solution)/shard_map/ppermute | solution.py:296
  8.4 4.7 %collective-permute-start.3 = (bf16[2,2,64,128]{3,2,1,0:T(8,128)(2,1)S(1)}, bf16[2,2,64,128]{3,2,1,0:T(8,128)(2,1)S(1)}, u32[]{:S(2)}, u32[]{:S(2)}) collective-permute-start(bf16[2,2,64,128]{3,2,1,0:T(8,128)(2,1)S(1)} %pad_maximum_fusion.1), channel_id=1, source_target_pairs={{0,2},{2,0},{1,3},{3,1},{4,6},{6,4},{5,7},{7,5},{8,10},{10,8},{9,1... | collective-permute-start | bytes 196616 | tf_op jit(solution)/shard_map/ppermute | solution.py:296
  11.3 5.6 %copy-start.1 = (bf16[2,128,128]{2,1,0:T(8,128)(2,1)S(1)}, bf16[2,128,128]{2,1,0:T(8,128)(2,1)}, u32[]{:S(2)}) copy-start(bf16[2,128,128]{2,1,0:T(8,128)(2,1)} %refs_8_.1) | copy-start | bytes 196612
  11.3 5.6 %copy-start.2 = (s32[32]{0:T(128)S(1)}, s32[32]{0:T(128)}, u32[]{:S(2)}) copy-start(s32[32]{0:T(128)} %refs_6_.1) | copy-start | bytes 388
  11.3 4.3 %collective-permute-start.4 = (bf16[2,2,64,128]{3,2,1,0:T(8,128)(2,1)S(1)}, bf16[2,2,64,128]{3,2,1,0:T(8,128)(2,1)S(1)}, u32[]{:S(2)}, u32[]{:S(2)}) collective-permute-start(bf16[2,2,64,128]{3,2,1,0:T(8,128)(2,1)S(1)} %pad_maximum_fusion.2), channel_id=1, source_target_pairs={{0,2},{2,0},{1,3},{3,1},{4,6},{6,4},{5,7},{7,5},{8,10},{10,8},{9,1... | collective-permute-start | bytes 196616 | tf_op jit(solution)/shard_map/ppermute | solution.py:296
  12.9 4.0 %collective-permute-start.5 = (bf16[4,2,64,128]{3,2,1,0:T(8,128)(2,1)S(1)}, bf16[4,2,64,128]{3,2,1,0:T(8,128)(2,1)S(1)}, u32[]{:S(2)}, u32[]{:S(2)}) collective-permute-start(bf16[4,2,64,128]{3,2,1,0:T(8,128)(2,1)S(1)} %pad_maximum_fusion.refs_0_), channel_id=1, source_target_pairs={{0,1},{1,0},{2,3},{3,2},{4,5},{5,4},{6,7},{7,6},{8,9},{9,8},{10,11... | collective-permute-start | bytes 393224 | tf_op jit(solution)/shard_map/ppermute | solution.py:296
  13.1 2.6 %collective-permute-start.6 = (bf16[2,2,64,128]{3,2,1,0:T(8,128)(2,1)S(1)}, bf16[2,2,64,128]{3,2,1,0:T(8,128)(2,1)S(1)}, u32[]{:S(2)}, u32[]{:S(2)}) collective-permute-start(bf16[2,2,64,128]{3,2,1,0:T(8,128)(2,1)S(1)} %collective-permute-done.3.refs_1_), channel_id=1, source_target_pairs={{0,1},{1,0},{2,3},{3,2},{4,5},{5,4},{6,7},{7,6},{8,9},{9,8},{10,11... | collective-permute-start | bytes 196616 | tf_op jit(solution)/shard_map/ppermute | solution.py:296
  15.7 1.3 %collective-permute-start.7 = (bf16[2,2,64,128]{3,2,1,0:T(8,128)(2,1)S(1)}, bf16[2,2,64,128]{3,2,1,0:T(8,128)(2,1)S(1)}, u32[]{:S(2)}, u32[]{:S(2)}) collective-permute-start(bf16[2,2,64,128]{3,2,1,0:T(8,128)(2,1)S(1)} %collective-permute-done.4.refs_2_), channel_id=1, source_target_pairs={{0,1},{1,0},{2,3},{3,2},{4,5},{5,4},{6,7},{7,6},{8,9},{9,8},{10,11... | collective-permute-start | bytes 196616 | tf_op jit(solution)/shard_map/ppermute | solution.py:296
